TPU v7x, 32 devices: a whole 2x2x4 slice. The times are simulated.
32 devices in a mesh: ctx: 4 (over y, x), head: 8 (over z, core).
Axes of the slice: x: 2, y: 2, z: 4, core: 2. Of those that a mesh axis runs over, the one named last changes fastest.
Arguments:
- queries: bfloat16 [256, 16384], P(None, 'head'), may hold values from -64 to 64, as said below
- grad_out: bfloat16 [256, 16384], P(None, 'head'), may hold values from -24 to 24
- latent: bfloat16 [8192, 512], P(('ctx', 'head')), may hold values from -6.1 to 6.1
- up_key: bfloat16 [512, 16384], P(None, 'head'), as said below
- up_value: bfloat16 [512, 16384], P(None, 'head'), may hold values from -0.25 to 0.25
Outputs:
- grad_queries: float32 [256, 16384], P('ctx', 'head')
- grad_latent: float32 [8192, 512], P(('ctx', 'head'))
- grad_up_key: float32 [512, 16384], P('ctx', 'head')
- grad_up_value: float32 [512, 16384], P('ctx', 'head')
Inputs may be any that keep to these rules, and one draw needn't show every extreme that they name: `queries`: entries lie within 64 in magnitude. `up_key`: entries lie within 4 / sqrt(512) in magnitude.
All inputs are finite; a program needn't handle non-finite values.
Results may differ from a plain program's by a relative error of at most 0.005.
Values may be sent and summed in bfloat16 or wider, within the bound.
No kernel may reach another device: no remote copies, remote signals or barrier semaphores. Data moves between devices by JAX's collectives and lax.ppermute only.
A program may use at most 128 MiB of HBM per device.

v0:
```python
import math

import jax
import jax.numpy as jnp
from jax import lax
from jax.sharding import PartitionSpec as P

HD = 128


def joined(part, axis, combine):
    gathered = jax.tree.map(lambda a: lax.all_gather(a, axis), part)

    def take(source):
        return jax.tree.map(lambda a: lax.dynamic_index_in_dim(a, source, 0, False), gathered)

    return lax.fori_loop(
        1, lax.axis_size(axis), lambda source, state: combine(state, take(source)), take(0)
    )


def join_triples(former, latter):
    maxima = jnp.maximum(former[0], latter[0])
    left_factor = jnp.exp(former[0] - maxima)
    right_factor = jnp.exp(latter[0] - maxima)
    return (
        maxima,
        former[1] * left_factor + latter[1] * right_factor,
        former[2] * left_factor + latter[2] * right_factor,
    )


def local(queries, grad_out, latent, up_key, up_value):
    scale = 1.0 / math.sqrt(HD)
    local_heads = queries.shape[1] // HD
    width = queries.shape[1]
    query_count = queries.shape[0]
    contract_cols = (((1,), (1,)), ((), ()))
    contract_rows = (((0,), (0,)), ((), ()))
    block = lax.all_gather(latent, "head", axis=0, tiled=True)
    key_rows = block.shape[0]
    total_len = key_rows * lax.axis_size("ctx")
    first_key = lax.axis_index("ctx") * key_rows
    key_block = jnp.dot(block, up_key, preferred_element_type=jnp.float32)
    value_block = jnp.dot(block, up_value, preferred_element_type=jnp.float32).astype(jnp.bfloat16)
    query_pos = total_len - query_count + lax.iota(jnp.int32, query_count)
    key_pos = first_key + lax.iota(jnp.int32, key_rows)
    visible = key_pos[None, :] <= query_pos[:, None]
    head_ids = jnp.arange(local_heads, dtype=jnp.int32)

    def head_inputs(head_index):
        offset = head_index * HD
        return (
            lax.dynamic_slice_in_dim(queries, offset, HD, 1),
            lax.dynamic_slice_in_dim(grad_out, offset, HD, 1),
            lax.dynamic_slice_in_dim(key_block, offset, HD, 1),
            lax.dynamic_slice_in_dim(value_block, offset, HD, 1),
        )

    def masked_scores(query_head, key_head):
        raw = (
            lax.dot_general(
                query_head.astype(jnp.float32),
                key_head,
                contract_cols,
                precision=lax.Precision.HIGHEST,
            )
            * scale
        )
        return jnp.where(visible, raw, -jnp.inf)

    def product_scores(grad_head, value_head):
        return lax.dot_general(
            grad_head, value_head, contract_cols, preferred_element_type=jnp.float32
        )

    def pick_row(table, head_index):
        return lax.dynamic_index_in_dim(table, head_index, 0, keepdims=False)

    def local_triple(head_index):
        query_head, grad_head, key_head, value_head = head_inputs(head_index)
        scores = masked_scores(query_head, key_head)
        maxima = jnp.max(scores, axis=1)
        weights = jnp.exp(scores - maxima[:, None])
        grad_probs = product_scores(grad_head, value_head)
        return (maxima, jnp.sum(weights, axis=1), jnp.sum(weights * grad_probs, axis=1))

    local_max, local_sum, local_weighted = lax.map(local_triple, head_ids)
    maxima, totals, weighted = joined((local_max, local_sum, local_weighted), "ctx", join_triples)
    deltas = weighted / totals

    def accumulate(head_index, carry):
        query_acc, grad_kv = carry
        query_head, grad_head, key_head, value_head = head_inputs(head_index)
        scores = masked_scores(query_head, key_head)
        probs = (
            jnp.exp(scores - pick_row(maxima, head_index)[:, None])
            / pick_row(totals, head_index)[:, None]
        )
        grad_probs = product_scores(grad_head, value_head)
        grad_scores = (probs * (grad_probs - pick_row(deltas, head_index)[:, None]) * scale).astype(
            jnp.bfloat16
        )
        query_part = jnp.dot(
            grad_scores.astype(jnp.float32), key_head, precision=lax.Precision.HIGHEST
        )
        key_grad = lax.dot_general(
            grad_scores, query_head, contract_rows, preferred_element_type=jnp.float32
        ).astype(jnp.bfloat16)
        value_grad = lax.dot_general(
            probs.astype(jnp.bfloat16), grad_head, contract_rows, preferred_element_type=jnp.float32
        ).astype(jnp.bfloat16)
        offset = head_index * HD
        anchor = jnp.zeros((), jnp.int32)
        query_acc = lax.dynamic_update_slice(query_acc, query_part, (anchor, offset))
        grad_kv = lax.dynamic_update_slice(grad_kv, key_grad, (anchor, offset))
        grad_kv = lax.dynamic_update_slice(grad_kv, value_grad, (anchor, width + offset))
        return (query_acc, grad_kv)

    start_state = (
        jnp.zeros((query_count, width), jnp.float32),
        jnp.zeros((key_rows, 2 * width), jnp.bfloat16),
    )
    query_acc, grad_kv = lax.fori_loop(0, local_heads, accumulate, start_state)
    up_both = jnp.concatenate([up_key, up_value], axis=1)
    grad_queries = lax.psum_scatter(query_acc, "ctx", scatter_dimension=0, tiled=True)
    weight_sums = lax.psum_scatter(
        lax.dot_general(block, grad_kv, contract_rows, preferred_element_type=jnp.float32),
        "ctx",
        scatter_dimension=0,
        tiled=True,
    )
    own_rows = latent.shape[0]
    summed = lax.psum(
        lax.dot_general(grad_kv, up_both, contract_cols, preferred_element_type=jnp.float32), "head"
    )
    grad_latent = lax.dynamic_slice_in_dim(summed, lax.axis_index("head") * own_rows, own_rows, 0)
    return (grad_queries, grad_latent, weight_sums[:, :width], weight_sums[:, width:])


def solution(mesh):
    return jax.shard_map(
        local,
        mesh=mesh,
        in_specs=(
            P(None, "head"),
            P(None, "head"),
            P(("ctx", "head"), None),
            P(None, "head"),
            P(None, "head"),
        ),
        out_specs=(P("ctx", "head"), P(("ctx", "head"), None), P("ctx", "head"), P("ctx", "head")),
        check_vma=False,
    )
```

profile of v0, /device:TPU:17, one launch (start us, length us, event | category | flops | bytes accessed | tf_op | source)
XLA Modules:
  0.0 606.5 jit_solution(6922244986778586002)
XLA Ops:
  8.0 31.7 %all-gather.5.cloned.1.call-done = bf16[2048,512]{1,0:T(8,128)(2,1)} async-done(((bf16[256,512]{1,0:T(8,128)(2,1)}), bf16[2048,512]{1,0:T(8,128)(2,1)}) %all-gather.5.cloned.1.call-update) | async-done | bytes 2097168 | tf_op jit(solution)/shard_map/all_gather | solution.py:40
  39.7 10.1 %convolution_convert_fusion.2 = bf16[2048,2048]{1,0:T(8,128)(2,1)} fusion(bf16[2048,512]{1,0:T(8,128)(2,1)} %all-gather.5.cloned.1.call-done, bf16[512,2048]{1,0:T(8,128)(2,1)} %param.15), kind=kOutput, calls=%fused_computation.52 | convolution fusion | flops 4299161600 | bytes 12582912 | tf_op jit(solution)/shard_map/dot_general | solution.py:45
  49.8 8.0 %fusion.45 = f32[2048,2048]{1,0:T(8,128)} fusion(bf16[2048,512]{1,0:T(8,128)(2,1)S(1)} %copy-done.2, bf16[512,2048]{1,0:T(8,128)(2,1)S(1)} %copy-done.1), kind=kOutput, calls=%fused_computation.64 | convolution fusion | flops 4294967296 | bytes 20971520 | tf_op jit(solution)/shard_map/dot_general | solution.py:44
  57.8 97.3 %while.53 = (s32[]{:T(128)}, f32[16,256]{1,0:T(8,128)S(1)}, f32[16,256]{1,0:T(8,128)S(1)}, f32[16,256]{1,0:T(8,128)S(1)}, s32[16]{0:T(128)S(1)}, /*index=5*/bf16...) while((s32[]{:T(128)}, f32[16,256]{1,0:T(8,128)S(1)}, ...), condition=%wide.region_4.5_spmd.clone, body=%wide.region_0.4_spmd.clone.sunk | while | flops 944241920 | bytes 8018139 | solution.py:88
  155.1 6.2 %all-gather.2 = f32[64,256]{1,0:T(8,128)S(1)} all-gather(f32[16,256]{1,0:T(8,128)S(1)} %get-tuple-element.503), channel_id=4, replica_groups=mesh['ctx'=4,'head'=8] {'ctx'}, dimensions={0}, use_global_device_ids=true | all-gather | bytes 81920 | tf_op jit(solution)/shard_map/all_gather | solution.py:12
  161.3 6.2 %all-gather = f32[64,256]{1,0:T(8,128)S(1)} all-gather(f32[16,256]{1,0:T(8,128)S(1)} %get-tuple-element.501), channel_id=2, replica_groups=mesh['ctx'=4,'head'=8] {'ctx'}, dimensions={0}, use_global_device_ids=true | all-gather | bytes 81920 | tf_op jit(solution)/shard_map/all_gather | solution.py:12
  167.5 5.4 all-gather.1
  173.5 6.0 broadcast_in_dim.43
  179.4 174.9 %while.54 = (s32[]{:T(128)}, f32[256,2048]{1,0:T(8,128)S(1)}, bf16[2048,4096]{1,0:T(8,128)(2,1)}, bf16[256,2048]{1,0:T(8,128)(2,1)}, f32[2048,2048]{1,0:T(8,128)...) while((s32[]{:T(128)}, f32[256,2048]{1,0:T(8,128)S(1)}, ...), condition=%wide.region_8.9_spmd.clone, body=%wide.region_7.8_spmd.clone.sunk | while | flops 2019033088 | bytes 13522222 | solution.py:124
  190.4 2.7 fusion.93
  201.3 2.7 fusion.93
  223.2 2.7 fusion.93
  234.1 2.7 fusion.93
  245.1 2.7 fusion.93
  256.0 2.7 fusion.93
  288.7 2.7 fusion.93
  299.7 2.7 fusion.93
  321.5 2.7 fusion.93
  332.5 2.7 fusion.93
  354.4 15.7 %fusion.38 = f32[2048,512]{1,0:T(8,128)} fusion(bf16[2048,4096]{1,0:T(8,128)(2,1)} %get-tuple-element.508, bf16[512,2048]{1,0:T(8,128)(2,1)} %param.15, bf16[512,2048]{1,0:T(8,128)(2,1)} %param.14), kind=kOutput, calls=%fused_computation.54 | convolution fusion | flops 8598323200 | bytes 25165824 | tf_op jit(solution)/shard_map/dot_general | solution.py:135
  371.7 14.5 %convolution_bitcast_fusion = f32[512,4096]{0,1:T(8,128)} fusion(bf16[2048,4096]{1,0:T(8,128)(2,1)} %get-tuple-element.508, bf16[2048,512]{1,0:T(8,128)(2,1)S(1)} %copy-done.3), kind=kOutput, calls=%fused_computation.53 | convolution fusion | flops 8589934592 | bytes 27262976 | tf_op jit(solution)/shard_map/dot_general | solution.py:128
  386.8 84.6 %all-reduce.2.cloned.1.call-done = f32[2048,512]{1,0:T(8,128)} async-done(((f32[2048,512]{1,0:T(8,128)}), f32[2048,512]{1,0:T(8,128)}) %all-reduce.2.cloned.1.call-update) | async-done | bytes 4194320 | tf_op jit(solution)/shard_map/psum | solution.py:134
  473.3 87.7 %reduce-scatter.5.cloned.1.call-done = f32[128,4096]{0,1:T(8,128)} async-done(((f32[512,4096]{0,1:T(8,128)}), f32[128,4096]{0,1:T(8,128)}) %reduce-scatter.5.cloned.1.call-update) | async-done | bytes 2097168 | tf_op jit(solution)/shard_map/reduce_scatter | solution.py:127
  565.3 34.6 %reduce-scatter.3.cloned.1.call-done = f32[64,2048]{1,0:T(8,128)} async-done(((f32[256,2048]{1,0:T(8,128)}), f32[64,2048]{1,0:T(8,128)}) %reduce-scatter.3.cloned.1.call-update) | async-done | bytes 524304 | tf_op jit(solution)/shard_map/reduce_scatter | solution.py:126
  (255 shorter events, 243.1 us)
Async XLA Ops:
  7.2 32.5 %all-gather.5.cloned.1.call-start = ((), (), s32[]{:S(2)}) async-start(), calls=%async_computation.2 | async-start | bytes 2359296 | tf_op jit(solution)/shard_map/all_gather | solution.py:40
  7.9 463.5 %all-reduce.2.cloned.1.call-start = ((), (), s32[]{:S(2)}) async-start(), calls=%async_computation.4 | async-start | bytes 8388608 | tf_op jit(solution)/shard_map/psum | solution.py:134
  39.7 10.1 %copy-start.1 = (bf16[512,2048]{1,0:T(8,128)(2,1)S(1)}, bf16[512,2048]{1,0:T(8,128)(2,1)}, u32[]{:S(2)}) copy-start(bf16[512,2048]{1,0:T(8,128)(2,1)} %param.14) | copy-start | bytes 6291460
  39.7 10.1 %copy-start.2 = (bf16[2048,512]{1,0:T(8,128)(2,1)S(1)}, bf16[2048,512]{1,0:T(8,128)(2,1)}, u32[]{:S(2)}) copy-start(bf16[2048,512]{1,0:T(8,128)(2,1)} %all-gather.5.cloned.1.call-done) | copy-start | bytes 6291460
  354.4 15.7 %copy-start = (f32[256,2048]{1,0:T(8,128)}, f32[256,2048]{1,0:T(8,128)S(1)}, u32[]{:S(2)}) copy-start(f32[256,2048]{1,0:T(8,128)S(1)} %get-tuple-element.507) | copy-start | bytes 6291460
  370.1 1.6 copy-start.3
  370.1 190.9 %reduce-scatter.5.cloned.1.call-start = ((), (), s32[]{:S(2)}) async-start(), calls=%async_computation.5 | async-start | bytes 10485760 | tf_op jit(solution)/shard_map/reduce_scatter | solution.py:127
  386.2 213.8 %reduce-scatter.3.cloned.1.call-start = ((), (), s32[]{:S(2)}) async-start(), calls=%async_computation.3 | async-start | bytes 2621440 | tf_op jit(solution)/shard_map/reduce_scatter | solution.py:126
Sparse Core Ops, SparseCore 0:
  9.6 30.0 all-gather.4
  370.2 101.1 all-reduce.1
  474.5 86.4 reduce-scatter.4
  564.7 35.2 reduce-scatter.2
where the time goes:
time: 612 us; the launch traced here: 606 us
  matrix products  291 us (48%)
  waiting for transfers between devices  240 us (39%)
  local copies, waits for them, and re-layouts  25.3 us (4%)
  blocking collectives  17.8 us (3%)
  between operations  13.9 us (2%)
  loops' own time  11.6 us (2%)
  other arithmetic  7.09 us (1%)
    reduce_scatter x1, waiting for transfers between devices, local(): lax.psum_scatter(lax.dot_general(block, grad_kv, contract_rows, preferred...  87.7 us
    dot_general x32, matrix products, masked_scores(): lax.dot_general(query_head.astype(jnp.float32), key_head, contract_cols,...  85 us
    psum x1, waiting for transfers between devices, local(): lax.psum(lax.dot_general(grad_kv, up_both, contract_cols, preferred_eleme...  84.6 us
    dot_general x32, matrix products, product_scores(): lax.dot_general(grad_head, value_head, contract_cols, preferred_element_t...  51.1 us
    dot_general x16, matrix products, accumulate(): jnp.dot(grad_scores.astype(jnp.float32), key_head, precision=lax.Precisio...  36.1 us
    dot_general x16, matrix products, accumulate(): lax.dot_general(grad_scores, query_head, contract_rows, preferred_element...  35.1 us
    dot_general x16, matrix products, accumulate(): lax.dot_general(probs.astype(jnp.bfloat16), grad_head, contract_rows, pre...  34.9 us
    reduce_scatter x1, waiting for transfers between devices, local(): lax.psum_scatter(query_acc, 'ctx', scatter_dimension=0, tiled=True)  34.6 us
  transfers between devices with their start and end apart: 4, of which 4 were waited for; matrix products, arithmetic and copies ran while one was open for 3% of the time, Pallas kernels for 0%

commit v1 on v0

v1 whole, which is shorter than its diff:
```python
import functools
import math

import jax
import jax.numpy as jnp
from jax import lax
from jax.experimental import pallas as pl
from jax.experimental.pallas import tpu as pltpu
from jax.sharding import PartitionSpec as P

HD = 128
GROUPS = 4
PAIR = 2
VMEM = 60 << 20
NT = (((1,), (1,)), ((), ()))
TN = (((0,), (0,)), ((), ()))
NN = (((1,), (0,)), ((), ()))
SCALE = 1.0 / math.sqrt(HD)
LOG2E = math.log2(math.e)
F32 = jnp.float32
BF16 = jnp.bfloat16


def dot(a, b, dims=NN):
    return lax.dot_general(a, b, dims, preferred_element_type=F32)


def swap(array, axis, distance):
    count = lax.axis_size(axis)
    return lax.ppermute(array, axis, [(i, i ^ distance) for i in range(count)])


def masked(s, gap):
    rows = lax.broadcasted_iota(jnp.int32, s.shape, 0)
    cols = lax.broadcasted_iota(jnp.int32, s.shape, 1)
    return jnp.where(rows - cols > gap, -jnp.inf, s)


def lanes(head):
    return slice(head * HD, (head + 1) * HD)


def join(parts):
    m = functools.reduce(jnp.maximum, [p[0] for p in parts])
    factors = [jnp.exp2(p[0] - m) for p in parts]
    t = sum(p[1] * f for p, f in zip(parts, factors))
    d = sum(p[2] * f for p, f in zip(parts, factors))
    return m, t, d


def triple(ref, head):
    return tuple(ref[3 * head + i : 3 * head + i + 1, :] for i in range(3))


def stats_kernel(chunk, gaps_ref, a_ref, b_ref, uk_ref, uv_ref, q_ref, do_ref, *refs):
    k2_ref, v_ref, latt_ref, st_ref = refs[-4:]
    rb = a_ref.shape[0]
    qn = q_ref.shape[0]
    pair = range(PAIR)
    weights = [jnp.concatenate([uk_ref[:, lanes(a)], uv_ref[:, lanes(a)]], axis=1) for a in pair]
    q = [q_ref[:, lanes(a)] for a in pair]
    qq = [jnp.concatenate([x, x], axis=1) for x in q]
    do = [do_ref[:, lanes(a)] for a in pair]
    parts = [[] if chunk == 0 else [triple(refs[0], a)] for a in pair]
    for side, lat_ref in enumerate((a_ref, b_ref)):
        rows = pl.ds(side * rb, rb)
        for a in pair:
            kv = dot(lat_ref[...], weights[a])
            k = kv[:, :HD] * (SCALE * LOG2E)
            hi = k.astype(BF16)
            lo = (k - hi.astype(F32)).astype(BF16)
            k2 = jnp.concatenate([hi, lo], axis=1)
            v = kv[:, HD:].astype(BF16)
            k2_ref[a, rows, :] = k2
            v_ref[a, rows, :] = v
            s = masked(dot(k2, qq[a], NT), gaps_ref[2 * chunk + side])
            gp = dot(v, do[a], NT)
            m = jnp.maximum(jnp.max(s, axis=0, keepdims=True), -1e30)
            w = jnp.exp2(s - m)
            parts[a].append((m, jnp.sum(w, axis=0, keepdims=True), jnp.sum(w * gp, axis=0, keepdims=True)))
    pad = jnp.zeros((8 - 3 * PAIR, qn), F32)
    st_ref[...] = jnp.concatenate([x for a in pair for x in join(parts[a])] + [pad], axis=0)

    @pl.when(pl.program_id(0) == 0)
    def _():
        latt_ref[:, 0:rb] = a_ref[...].T
        latt_ref[:, rb : 2 * rb] = b_ref[...].T


def run_stats(chunk, gaps, a, b, up_key, up_value, queries, grad_out, before):
    rb, depth = a.shape
    heads = queries.shape[1] // HD
    qn = queries.shape[0]
    wide = PAIR * HD
    col = lambda g, *_: (0, g)
    whole = pl.BlockSpec((rb, depth), lambda g, *_: (0, 0))
    st_spec = pl.BlockSpec((None, 8, qn), lambda g, *_: (g, 0, 0))
    extra = () if before is None else (before,)
    return pl.pallas_call(
        functools.partial(stats_kernel, chunk),
        out_shape=(
            jax.ShapeDtypeStruct((heads, 2 * rb, 2 * HD), BF16),
            jax.ShapeDtypeStruct((heads, 2 * rb, HD), BF16),
            jax.ShapeDtypeStruct((depth, 2 * rb), BF16),
            jax.ShapeDtypeStruct((heads // PAIR, 8, qn), F32),
        ),
        grid_spec=pltpu.PrefetchScalarGridSpec(
            num_scalar_prefetch=1,
            grid=(heads // PAIR,),
            in_specs=[
                whole,
                whole,
                pl.BlockSpec((depth, wide), col),
                pl.BlockSpec((depth, wide), col),
                pl.BlockSpec((qn, wide), col),
                pl.BlockSpec((qn, wide), col),
            ]
            + [st_spec] * len(extra),
            out_specs=[
                pl.BlockSpec((PAIR, 2 * rb, 2 * HD), lambda g, *_: (g, 0, 0)),
                pl.BlockSpec((PAIR, 2 * rb, HD), lambda g, *_: (g, 0, 0)),
                pl.BlockSpec((depth, 2 * rb), lambda g, *_: (0, 0)),
                st_spec,
            ],
        ),
        compiler_params=pltpu.CompilerParams(vmem_limit_bytes=VMEM),
        cost_estimate=pl.CostEstimate(
            flops=heads * 2 * rb * HD * 2 * (2 * depth + 4 * qn),
            bytes_accessed=heads * 2 * rb * HD * 6,
            transcendentals=heads * 2 * rb * qn,
        ),
        name="stats",
    )(gaps, a, b, up_key, up_value, queries, grad_out, *extra)


def grads_kernel(n, chunks, gaps_ref, q_ref, do_ref, st_ref, *refs):
    k2_refs, v_refs = refs[:chunks], refs[chunks : 2 * chunks]
    gk_ref, gv_ref, gq_ref = refs[2 * chunks :]
    rows2 = k2_refs[0].shape[1]
    rb = rows2 // 2
    qn = q_ref.shape[0]
    pair = range(PAIR)
    q = [q_ref[:, lanes(a)] for a in pair]
    qq = [jnp.concatenate([x, x], axis=1) for x in q]
    do = [do_ref[:, lanes(a)] for a in pair]
    shift, delta = [], []
    for a in pair:
        m, t, d = join([triple(st_ref.at[i], a) for i in range(n)])
        shift.append(m + jnp.log2(t))
        delta.append(d / t)
    gq = [jnp.zeros((qn, 2 * HD), F32) for a in pair]
    for c in range(chunks):
        rows = pl.ds(c * rows2, rows2)
        for a in pair:
            k2 = k2_refs[c][a]
            s = dot(k2, qq[a], NT)
            s = jnp.concatenate([masked(s[:rb], gaps_ref[2 * c]), masked(s[rb:], gaps_ref[2 * c + 1])], axis=0)
            gp = dot(v_refs[c][a], do[a], NT)
            p = jnp.exp2(s - shift[a])
            ds = (p * (gp - delta[a]) * SCALE).astype(BF16)
            low = p.astype(BF16)
            gk_ref[rows, lanes(a)] = dot(ds, q[a]).astype(BF16)
            gv_ref[rows, lanes(a)] = dot(low, do[a]).astype(BF16)
            gq[a] = gq[a] + dot(ds, k2, TN)
    for a in pair:
        gq_ref[:, lanes(a)] = (gq[a][:, :HD] + gq[a][:, HD:]) * (1.0 / (SCALE * LOG2E))


def run_grads(gaps, queries, grad_out, k2, v, stats, first_head, per):
    chunks = len(k2)
    n = stats.shape[0]
    rows2 = k2[0].shape[1]
    rows = chunks * rows2
    qn = queries.shape[0]
    wide = PAIR * HD
    base = first_head // PAIR
    col = lambda g, *_: (0, base + g)
    out = lambda g, *_: (0, g)
    return pl.pallas_call(
        functools.partial(grads_kernel, n, chunks),
        out_shape=(
            jax.ShapeDtypeStruct((rows, per * HD), BF16),
            jax.ShapeDtypeStruct((rows, per * HD), BF16),
            jax.ShapeDtypeStruct((qn, per * HD), F32),
        ),
        grid_spec=pltpu.PrefetchScalarGridSpec(
            num_scalar_prefetch=1,
            grid=(per // PAIR,),
            in_specs=[
                pl.BlockSpec((qn, wide), col),
                pl.BlockSpec((qn, wide), col),
                pl.BlockSpec((n, None, 8, qn), lambda g, *_: (0, base + g, 0, 0)),
            ]
            + [pl.BlockSpec((PAIR, rows2, 2 * HD), lambda g, *_: (base + g, 0, 0))] * chunks
            + [pl.BlockSpec((PAIR, rows2, HD), lambda g, *_: (base + g, 0, 0))] * chunks,
            out_specs=[
                pl.BlockSpec((rows, wide), out),
                pl.BlockSpec((rows, wide), out),
                pl.BlockSpec((qn, wide), out),
            ],
        ),
        compiler_params=pltpu.CompilerParams(vmem_limit_bytes=VMEM),
        cost_estimate=pl.CostEstimate(
            flops=per * rows * HD * 2 * 7 * qn,
            bytes_accessed=per * rows * HD * 10,
            transcendentals=per * rows * qn,
        ),
        name="grads",
    )(gaps, queries, grad_out, stats, *k2, *v)


def ups_kernel(n, chunks, gk_ref, gv_ref, gq_ref, *refs):
    latt_refs, out_ref = refs[:chunks], refs[chunks]
    step = pl.program_id(0)
    depth, rows2 = latt_refs[0].shape
    rb, qb = depth // n, gq_ref.shape[0] // n
    wide = gk_ref.shape[1]
    half = out_ref.shape[2] // 2
    for side, ref in enumerate((gk_ref, gv_ref)):
        cols = pl.ds(pl.multiple_of(side * half + step * wide, wide), wide)
        gu = sum(dot(latt_refs[c][...], ref[pl.ds(c * rows2, rows2), :]) for c in range(chunks))
        for r in range(n):
            out_ref[r, 0:rb, cols] = gu[r * rb : (r + 1) * rb].astype(BF16)
            part = pl.ds(r * qb + side * (qb // 2), qb // 2)
            out_ref[r, rb : rb + qb // 2, cols] = gq_ref[part, :].astype(BF16)


def run_ups(n, latt, gk, gv, gq):
    chunks = len(latt)
    depth, rows2 = latt[0].shape
    rows, cols = gk.shape
    qn = gq.shape[0]
    wide = PAIR * HD
    shape = (n, depth // n + qn // n // 2, 2 * cols)
    block = lambda g: (0, g)
    return pl.pallas_call(
        functools.partial(ups_kernel, n, chunks),
        out_shape=jax.ShapeDtypeStruct(shape, BF16),
        grid=(cols // wide,),
        in_specs=[
            pl.BlockSpec((rows, wide), block),
            pl.BlockSpec((rows, wide), block),
            pl.BlockSpec((qn, wide), block),
        ]
        + [pl.BlockSpec((depth, rows2), lambda g: (0, 0))] * chunks,
        out_specs=pl.BlockSpec(shape, lambda g: (0, 0, 0)),
        compiler_params=pltpu.CompilerParams(vmem_limit_bytes=VMEM),
        cost_estimate=pl.CostEstimate(
            flops=4 * depth * rows * cols, bytes_accessed=4 * rows * cols, transcendentals=0
        ),
        name="ups",
    )(gk, gv, gq, *latt)


def latent_kernel(groups, uk_ref, uv_ref, *refs):
    keep_ref, send_ref = refs[-2:]
    per = refs[0].shape[1]
    total = None
    for g in range(groups):
        for w_ref, ref in ((uk_ref, refs[2 * g]), (uv_ref, refs[2 * g + 1])):
            term = dot(ref[...], w_ref[:, g * per : (g + 1) * per], NT)
            total = term if total is None else total + term
    rb = keep_ref.shape[0]
    keep_ref[...] = total[:rb].astype(BF16)
    send_ref[...] = total[rb:].astype(BF16)


def run_latent(up_key, up_value, gkv, rb):
    depth, width = up_key.shape
    rows, per = gkv[0].shape
    steps = rows // (2 * rb)
    whole = pl.BlockSpec((depth, width), lambda i: (0, 0))
    out = jax.ShapeDtypeStruct((steps, rb, depth), BF16)
    out_spec = pl.BlockSpec((None, rb, depth), lambda i: (i, 0, 0))
    return pl.pallas_call(
        functools.partial(latent_kernel, len(gkv) // 2),
        out_shape=(out, out),
        grid=(steps,),
        in_specs=[whole, whole] + [pl.BlockSpec((2 * rb, per), lambda i: (i, 0))] * len(gkv),
        out_specs=[out_spec, out_spec],
        compiler_params=pltpu.CompilerParams(vmem_limit_bytes=VMEM),
        cost_estimate=pl.CostEstimate(
            flops=4 * rows * depth * width, bytes_accessed=4 * rows * width, transcendentals=0
        ),
        name="latents",
    )(up_key, up_value, *gkv)


def local(queries, grad_out, latent, up_key, up_value):
    heads = queries.shape[1] // HD
    qn = queries.shape[0]
    n = lax.axis_size("ctx")
    mates = lax.axis_size("head")
    rb, depth = latent.shape
    chunks = mates // 2

    firsts = [latent] + [swap(latent, "head", 2 * k) for k in range(1, chunks)]
    seconds = [swap(x, "head", 1) for x in firsts]
    starts = (lax.axis_index("ctx") * mates + (lax.axis_index("head") ^ jnp.arange(mates))) * rb
    gaps = (rb * mates * n - qn - starts).astype(jnp.int32)
    k2, v, latt, stats = [], [], [], None
    for c in range(chunks):
        one_k2, one_v, one_latt, stats = run_stats(
            c, gaps, firsts[c], seconds[c], up_key, up_value, queries, grad_out, stats
        )
        k2.append(one_k2)
        v.append(one_v)
        latt.append(one_latt)
    stats = jnp.stack([stats] + [swap(stats, "ctx", k) for k in range(1, n)])

    per = heads // GROUPS
    gkv, gqs, outs = [], [], []

    def send(g):
        part = run_ups(n, latt, gkv[2 * g], gkv[2 * g + 1], gqs[g])
        outs.append(lax.all_to_all(part, "ctx", 0, 0, tiled=True))

    for g in range(GROUPS):
        gk, gv, gq = run_grads(gaps, queries, grad_out, k2, v, stats, g * per, per)
        gkv += [gk, gv]
        gqs.append(gq)
        if g < GROUPS // 2:
            send(g)
    keep, away = run_latent(up_key, up_value, gkv, rb)
    for g in range(GROUPS // 2, GROUPS):
        send(g)
    both = keep.astype(F32) + swap(away, "head", 1).astype(F32)
    low = both.astype(BF16)
    grad_latent = both[0]
    for k in range(1, chunks):
        grad_latent = grad_latent + swap(low[k], "head", 2 * k).astype(F32)

    sums = [jnp.sum(o.astype(F32), axis=0) for o in outs]
    ub = depth // n
    cols = per * HD
    grad_key = jnp.concatenate([s[:ub, :cols] for s in sums], axis=1)
    grad_value = jnp.concatenate([s[:ub, cols:] for s in sums], axis=1)
    grad_q = jnp.concatenate([jnp.concatenate([s[ub:, :cols], s[ub:, cols:]], axis=0) for s in sums], axis=1)
    return (grad_q, grad_latent, grad_key, grad_value)


def solution(mesh):
    return jax.shard_map(
        local,
        mesh=mesh,
        in_specs=(
            P(None, "head"),
            P(None, "head"),
            P(("ctx", "head"), None),
            P(None, "head"),
            P(None, "head"),
        ),
        out_specs=(P("ctx", "head"), P(("ctx", "head"), None), P("ctx", "head"), P("ctx", "head")),
        check_vma=False,
    )
```

time: 612 us -> 239 us (0.39)
  the two profiles are of different devices: /device:TPU:17 before, /device:TPU:0 now
where the time goes in v1:
time: 239 us; the launch traced here: 237 us
  Pallas kernels  132 us (55%)
  waiting for transfers between devices  56.7 us (24%)
  starting transfers between devices  33 us (14%)
  other arithmetic  9.48 us (4%)
  local copies, waits for them, and re-layouts  5.37 us (2%)
    pallas_call x4, Pallas kernels, run_stats(): pl.pallas_call(functools.partial(stats_kernel, chunk), out_shape=(jax.Sha...  49.7 us
    pallas_call x4, Pallas kernels, run_grads(): pl.pallas_call(functools.partial(grads_kernel, n, chunks), out_shape=(jax...  42.4 us
    ppermute x14, waiting for transfers between devices, swap(): return lax.ppermute(array, axis, [(i, i ^ distance) for i in range(count)])  42.4 us
    pallas_call x4, Pallas kernels, run_ups(): pl.pallas_call(functools.partial(ups_kernel, n, chunks), out_shape=jax.Sh...  25 us
    ppermute x14, starting transfers between devices, swap(): return lax.ppermute(array, axis, [(i, i ^ distance) for i in range(count)])  16.6 us
    all_to_all x4, starting transfers between devices, send(): outs.append(lax.all_to_all(part, 'ctx', 0, 0, tiled=True))  16.4 us
    pallas_call x1, Pallas kernels, run_latent(): pl.pallas_call(functools.partial(latent_kernel, len(gkv) // 2), out_shape...  14.4 us
    all_to_all x4, waiting for transfers between devices, send(): outs.append(lax.all_to_all(part, 'ctx', 0, 0, tiled=True))  14.3 us
  transfers between devices with their start and end apart: 18, of which 9 were waited for; matrix products, arithmetic and copies ran while one was open for 3% of the time, Pallas kernels for 43%

profile of v1, /device:TPU:0, one launch (start us, length us, event | category | flops | bytes accessed | tf_op | source)
XLA Modules:
  0.0 237.1 jit_solution(6372225194675596133)
XLA Ops:
  0.6 3.1 %collective-permute-start.4 = (bf16[256,512]{1,0:T(8,128)(2,1)}, bf16[256,512]{1,0:T(8,128)(2,1)S(1)}, u32[]{:S(2)}, u32[]{:S(2)}) collective-permute-start(bf16[256,512]{1,0:T(8,128)(2,1)} %a_ref.1), channel_id=1, source_target_pairs={{0,2},{1,3},{2,0},{3,1},{4,6},{5,7},{6,4},{7,5},{8,10},{9,11},{10,... | collective-permute-start | bytes 786440 | tf_op jit(solution)/shard_map/ppermute | solution.py:30
  6.8 8.2 %collective-permute-done.4.a_ref = bf16[256,512]{1,0:T(8,128)(2,1)S(1)} collective-permute-done((bf16[256,512]{1,0:T(8,128)(2,1)}, bf16[256,512]{1,0:T(8,128)(2,1)S(1)}, u32[]{:S(2)}, u32[]{:S(2)}) %collective-permute-start.4) | collective-permute-done | bytes 262176 | tf_op jit(solution)/shard_map/ppermute | solution.py:30
  15.1 10.2 %collective-permute-done.2.a_ref = bf16[256,512]{1,0:T(8,128)(2,1)S(1)} collective-permute-done((bf16[256,512]{1,0:T(8,128)(2,1)}, bf16[256,512]{1,0:T(8,128)(2,1)S(1)}, u32[]{:S(2)}, u32[]{:S(2)}) %collective-permute-start.2) | collective-permute-done | bytes 262176 | tf_op jit(solution)/shard_map/ppermute | solution.py:30
  26.5 12.3 %stats.4 = (bf16[16,512,256]{2,1,0:T(8,128)(2,1)}, bf16[16,512,128]{2,1,0:T(8,128)(2,1)}, bf16[512,512]{1,0:T(8,128)(2,1)}, f32[8,8,256]{2,1,0:T(8,128)}) custom-call(s32[8]{0:T(128)} %multiply_subtract_fusion.gaps_ref, bf16[256,512]{1,0:T(8,128)(2,1)} %a_ref.1, bf16[256,512]{1,0:T(8,128)(2,1)} %copy-done.8, bf16[512,2048]{1,0:T(8,128)(2,1)} %uk_ref.9, ...), custom_call_target="tpu_custom_call" | custom-call | flops 4294967296 | bytes 6291456 | tf_op jit(solution)/shard_map/stats/pallas_call | solution.py:99
  39.6 12.5 %stats.5 = (bf16[16,512,256]{2,1,0:T(8,128)(2,1)}, bf16[16,512,128]{2,1,0:T(8,128)(2,1)}, bf16[512,512]{1,0:T(8,128)(2,1)}, f32[8,8,256]{2,1,0:T(8,128)}) custom-call(s32[8]{0:T(128)} %multiply_subtract_fusion.gaps_ref, bf16[256,512]{1,0:T(8,128)(2,1)} %copy-done.7, bf16[256,512]{1,0:T(8,128)(2,1)} %copy-done.11, bf16[512,2048]{1,0:T(8,128)(2,1)} %uk_ref.9, ...), custom_call_target="tpu_custom_call" | custom-call | flops 4294967296 | bytes 6291456 | tf_op jit(solution)/shard_map/stats/pallas_call | solution.py:99
  52.8 12.5 %stats.6 = (bf16[16,512,256]{2,1,0:T(8,128)(2,1)}, bf16[16,512,128]{2,1,0:T(8,128)(2,1)}, bf16[512,512]{1,0:T(8,128)(2,1)}, f32[8,8,256]{2,1,0:T(8,128)}) custom-call(s32[8]{0:T(128)} %multiply_subtract_fusion.gaps_ref, bf16[256,512]{1,0:T(8,128)(2,1)} %copy-done.6, bf16[256,512]{1,0:T(8,128)(2,1)} %copy-done.10, bf16[512,2048]{1,0:T(8,128)(2,1)} %uk_ref.9, ...), custom_call_target="tpu_custom_call" | custom-call | flops 4294967296 | bytes 6291456 | tf_op jit(solution)/shard_map/stats/pallas_call | solution.py:99
  66.0 12.5 %stats.7 = (bf16[16,512,256]{2,1,0:T(8,128)(2,1)}, bf16[16,512,128]{2,1,0:T(8,128)(2,1)}, bf16[512,512]{1,0:T(8,128)(2,1)}, f32[8,8,256]{2,1,0:T(8,128)}) custom-call(s32[8]{0:T(128)} %multiply_subtract_fusion.gaps_ref, bf16[256,512]{1,0:T(8,128)(2,1)} %copy-done.5, bf16[256,512]{1,0:T(8,128)(2,1)} %copy-done.9, bf16[512,2048]{1,0:T(8,128)(2,1)} %uk_ref.9, ...), custom_call_target="tpu_custom_call" | custom-call | flops 4294967296 | bytes 6291456 | tf_op jit(solution)/shard_map/stats/pallas_call | solution.py:99
  87.5 10.6 %grads.7 = (bf16[2048,512]{1,0:T(8,128)(2,1)}, bf16[2048,512]{1,0:T(8,128)(2,1)}, f32[256,512]{1,0:T(8,128)}) custom-call(s32[8]{0:T(128)} %multiply_subtract_fusion.gaps_ref, bf16[256,2048]{1,0:T(8,128)(2,1)} %q_ref.15, bf16[256,2048]{1,0:T(8,128)(2,1)} %do_ref.15, f32[4,8,8,256]{3,2,1,0:T(8,128)} %pad_maximum_fusion.2.st_ref, ...), custom_call_target="tpu_custom_call" | custom-call | flops 3758096384 | bytes 10485760 | tf_op jit(solution)/shard_map/grads/pallas_call | solution.py:179
  98.1 6.2 %ups.7 = bf16[4,160,1024]{2,1,0:T(8,128)(2,1)} custom-call(bf16[2048,512]{1,0:T(8,128)(2,1)} %get-tuple-element.59.gk_ref.refs_6_, bf16[2048,512]{1,0:T(8,128)(2,1)} %get-tuple-element.60.gv_ref.refs_7_, f32[256,512]{1,0:T(8,128)} %get-tuple-element.61.gq_ref, bf16[512,512]{1,0:T(8,128)(2,1)} %get-tuple-element.49.refs_0_, ...), custom_call_target="tpu_custom_call" | custom-call | flops 2147483648 | bytes 4194304 | tf_op jit(solution)/shard_map/ups/pallas_call | solution.py:236
  104.3 3.7 %all-to-all-start.3 = ((bf16[4,160,1024]{2,1,0:T(8,128)(2,1)}), bf16[4,160,1024]{2,1,0:T(8,128)(2,1)S(1)}, u32[]{:S(2)}, u32[]{:S(2)}) async-start(bf16[4,160,1024]{2,1,0:T(8,128)(2,1)} %ups.7), calls=%async_computation.3 | async-start | bytes 2621440 | tf_op jit(solution)/shard_map/all_to_all | solution.py:316
  108.1 10.6 %grads.6 = (bf16[2048,512]{1,0:T(8,128)(2,1)}, bf16[2048,512]{1,0:T(8,128)(2,1)}, f32[256,512]{1,0:T(8,128)}) custom-call(s32[8]{0:T(128)} %multiply_subtract_fusion.gaps_ref, bf16[256,2048]{1,0:T(8,128)(2,1)} %q_ref.15, bf16[256,2048]{1,0:T(8,128)(2,1)} %do_ref.15, f32[4,8,8,256]{3,2,1,0:T(8,128)} %pad_maximum_fusion.2.st_ref, ...), custom_call_target="tpu_custom_call" | custom-call | flops 3758096384 | bytes 10485760 | tf_op jit(solution)/shard_map/grads/pallas_call | solution.py:179
  118.6 6.2 %ups.6 = bf16[4,160,1024]{2,1,0:T(8,128)(2,1)} custom-call(bf16[2048,512]{1,0:T(8,128)(2,1)} %get-tuple-element.56.gk_ref.refs_4_, bf16[2048,512]{1,0:T(8,128)(2,1)} %get-tuple-element.57.gv_ref.refs_5_, f32[256,512]{1,0:T(8,128)} %get-tuple-element.58.gq_ref, bf16[512,512]{1,0:T(8,128)(2,1)} %get-tuple-element.49.refs_0_, ...), custom_call_target="tpu_custom_call" | custom-call | flops 2147483648 | bytes 4194304 | tf_op jit(solution)/shard_map/ups/pallas_call | solution.py:236
  124.9 4.0 %all-to-all-start.2 = ((bf16[4,160,1024]{2,1,0:T(8,128)(2,1)}), bf16[4,160,1024]{2,1,0:T(8,128)(2,1)S(1)}, u32[]{:S(2)}, u32[]{:S(2)}) async-start(bf16[4,160,1024]{2,1,0:T(8,128)(2,1)} %ups.6), calls=%async_computation.2 | async-start | bytes 2621440 | tf_op jit(solution)/shard_map/all_to_all | solution.py:316
  128.8 10.6 %grads.4 = (bf16[2048,512]{1,0:T(8,128)(2,1)}, bf16[2048,512]{1,0:T(8,128)(2,1)}, f32[256,512]{1,0:T(8,128)}) custom-call(s32[8]{0:T(128)} %multiply_subtract_fusion.gaps_ref, bf16[256,2048]{1,0:T(8,128)(2,1)} %q_ref.15, bf16[256,2048]{1,0:T(8,128)(2,1)} %do_ref.15, f32[4,8,8,256]{3,2,1,0:T(8,128)} %pad_maximum_fusion.2.st_ref, ...), custom_call_target="tpu_custom_call" | custom-call | flops 3758096384 | bytes 10485760 | tf_op jit(solution)/shard_map/grads/pallas_call | solution.py:179
  139.4 6.3 %ups.4 = bf16[4,160,1024]{2,1,0:T(8,128)(2,1)} custom-call(bf16[2048,512]{1,0:T(8,128)(2,1)} %get-tuple-element.46.gk_ref.refs_0_, bf16[2048,512]{1,0:T(8,128)(2,1)} %get-tuple-element.47.gv_ref.refs_1_, f32[256,512]{1,0:T(8,128)} %get-tuple-element.48.gq_ref, bf16[512,512]{1,0:T(8,128)(2,1)} %get-tuple-element.49.refs_0_, ...), custom_call_target="tpu_custom_call" | custom-call | flops 2147483648 | bytes 4194304 | tf_op jit(solution)/shard_map/ups/pallas_call | solution.py:236
  145.7 10.7 %grads.5 = (bf16[2048,512]{1,0:T(8,128)(2,1)}, bf16[2048,512]{1,0:T(8,128)(2,1)}, f32[256,512]{1,0:T(8,128)}) custom-call(s32[8]{0:T(128)} %multiply_subtract_fusion.gaps_ref, bf16[256,2048]{1,0:T(8,128)(2,1)} %q_ref.15, bf16[256,2048]{1,0:T(8,128)(2,1)} %do_ref.15, f32[4,8,8,256]{3,2,1,0:T(8,128)} %pad_maximum_fusion.2.st_ref, ...), custom_call_target="tpu_custom_call" | custom-call | flops 3758096384 | bytes 10485760 | tf_op jit(solution)/shard_map/grads/pallas_call | solution.py:179
  156.4 4.5 %all-to-all-start = ((bf16[4,160,1024]{2,1,0:T(8,128)(2,1)}), bf16[4,160,1024]{2,1,0:T(8,128)(2,1)}, u32[]{:S(2)}, u32[]{:S(2)}) async-start(bf16[4,160,1024]{2,1,0:T(8,128)(2,1)} %ups.4), calls=%async_computation | async-start | bytes 2621440 | tf_op jit(solution)/shard_map/all_to_all | solution.py:316
  161.0 14.4 %latents.1 = (bf16[4,256,512]{2,1,0:T(8,128)(2,1)}, bf16[4,256,512]{2,1,0:T(8,128)(2,1)}) custom-call(bf16[512,2048]{1,0:T(8,128)(2,1)} %uk_ref.9, bf16[512,2048]{1,0:T(8,128)(2,1)} %uv_ref.9, bf16[2048,512]{1,0:T(8,128)(2,1)} %get-tuple-element.46.gk_ref.refs_0_, bf16[2048,512]{1,0:T(8,128)(2,1)} %get-tuple-element.47.gv_ref.refs_1_, ...), custom_call_target="tpu_custom_call" | custom-call | flops 8589934592 | bytes 16777216 | tf_op jit(solution)/shard_map/latents/pallas_call | solution.py:275
  175.5 6.3 %ups.5 = bf16[4,160,1024]{2,1,0:T(8,128)(2,1)} custom-call(bf16[2048,512]{1,0:T(8,128)(2,1)} %get-tuple-element.53.gk_ref.refs_2_, bf16[2048,512]{1,0:T(8,128)(2,1)} %get-tuple-element.54.gv_ref.refs_3_, f32[256,512]{1,0:T(8,128)} %get-tuple-element.55.gq_ref, bf16[512,512]{1,0:T(8,128)(2,1)} %get-tuple-element.49.refs_0_, ...), custom_call_target="tpu_custom_call" | custom-call | flops 2147483648 | bytes 4194304 | tf_op jit(solution)/shard_map/ups/pallas_call | solution.py:236
  182.0 4.2 %all-to-all-start.1 = ((bf16[4,160,1024]{2,1,0:T(8,128)(2,1)}), bf16[4,160,1024]{2,1,0:T(8,128)(2,1)S(1)}, u32[]{:S(2)}, u32[]{:S(2)}) async-start(bf16[4,160,1024]{2,1,0:T(8,128)(2,1)} %ups.5), calls=%async_computation.1 | async-start | bytes 2621440 | tf_op jit(solution)/shard_map/all_to_all | solution.py:316
  189.0 14.3 %all-to-all-done.1 = bf16[4,160,1024]{2,1,0:T(8,128)(2,1)S(1)} async-done(((bf16[4,160,1024]{2,1,0:T(8,128)(2,1)}), bf16[4,160,1024]{2,1,0:T(8,128)(2,1)S(1)}, u32[]{:S(2)}, u32[]{:S(2)}) %all-to-all-start.1) | async-done | bytes 1310752 | tf_op jit(solution)/shard_map/all_to_all | solution.py:316
  207.9 4.4 %collective-permute-start.11 = (bf16[256,512]{1,0:T(8,128)(2,1)S(1)}, bf16[256,512]{1,0:T(8,128)(2,1)S(1)}, u32[]{:S(2)}, u32[]{:S(2)}) collective-permute-start(bf16[256,512]{1,0:T(8,128)(2,1)S(1)} %get-tuple-element.66), channel_id=1, source_target_pairs={{0,2},{1,3},{2,0},{3,1},{4,6},{5,7},{6,4},{7,5},{8,10},{9,11},{10,... | collective-permute-start | bytes 786440 | tf_op jit(solution)/shard_map/ppermute | solution.py:30
  219.0 8.6 %collective-permute-done.13 = bf16[256,512]{1,0:T(8,128)(2,1)S(1)} collective-permute-done((bf16[256,512]{1,0:T(8,128)(2,1)S(1)}, bf16[256,512]{1,0:T(8,128)(2,1)S(1)}, u32[]{:S(2)}, u32[]{:S(2)}) %collective-permute-start.13) | collective-permute-done | bytes 262176 | tf_op jit(solution)/shard_map/ppermute | solution.py:30
  227.6 8.6 %collective-permute-done.12 = bf16[256,512]{1,0:T(8,128)(2,1)S(1)} collective-permute-done((bf16[256,512]{1,0:T(8,128)(2,1)S(1)}, bf16[256,512]{1,0:T(8,128)(2,1)S(1)}, u32[]{:S(2)}, u32[]{:S(2)}) %collective-permute-start.12) | collective-permute-done | bytes 262176 | tf_op jit(solution)/shard_map/ppermute | solution.py:30
  (68 shorter events, 30.8 us)
Async XLA Ops:
  0.6 14.5 %collective-permute-start.4 = (bf16[256,512]{1,0:T(8,128)(2,1)}, bf16[256,512]{1,0:T(8,128)(2,1)S(1)}, u32[]{:S(2)}, u32[]{:S(2)}) collective-permute-start(bf16[256,512]{1,0:T(8,128)(2,1)} %a_ref.1), channel_id=1, source_target_pairs={{0,2},{1,3},{2,0},{3,1},{4,6},{5,7},{6,4},{7,5},{8,10},{9,11},{10,... | collective-permute-start | bytes 786440 | tf_op jit(solution)/shard_map/ppermute | solution.py:30
  3.7 21.6 %collective-permute-start.2 = (bf16[256,512]{1,0:T(8,128)(2,1)}, bf16[256,512]{1,0:T(8,128)(2,1)S(1)}, u32[]{:S(2)}, u32[]{:S(2)}) collective-permute-start(bf16[256,512]{1,0:T(8,128)(2,1)} %a_ref.1), channel_id=1, source_target_pairs={{0,4},{1,5},{2,6},{3,7},{4,0},{5,1},{6,2},{7,3},{8,12},{9,13},{10,... | collective-permute-start | bytes 786440 | tf_op jit(solution)/shard_map/ppermute | solution.py:30
  6.3 19.0 %collective-permute-start = (bf16[256,512]{1,0:T(8,128)(2,1)}, bf16[256,512]{1,0:T(8,128)(2,1)S(1)}, u32[]{:S(2)}, u32[]{:S(2)}) collective-permute-start(bf16[256,512]{1,0:T(8,128)(2,1)} %a_ref.1), channel_id=1, source_target_pairs={{0,6},{1,7},{2,4},{3,5},{4,2},{5,3},{6,0},{7,1},{8,14},{9,15},{10,... | collective-permute-start | bytes 786440 | tf_op jit(solution)/shard_map/ppermute | solution.py:30
  6.3 19.5 %collective-permute-start.6 = (bf16[256,512]{1,0:T(8,128)(2,1)}, bf16[256,512]{1,0:T(8,128)(2,1)S(1)}, u32[]{:S(2)}, u32[]{:S(2)}) collective-permute-start(bf16[256,512]{1,0:T(8,128)(2,1)} %a_ref.1), channel_id=1, source_target_pairs={{0,1},{1,0},{2,3},{3,2},{4,5},{5,4},{6,7},{7,6},{8,9},{9,8},{10,11... | collective-permute-start | bytes 786440 | tf_op jit(solution)/shard_map/ppermute | solution.py:30
  15.1 23.8 %copy-start.7 = (bf16[256,512]{1,0:T(8,128)(2,1)}, bf16[256,512]{1,0:T(8,128)(2,1)S(1)}, u32[]{:S(2)}) copy-start(bf16[256,512]{1,0:T(8,128)(2,1)S(1)} %collective-permute-done.4.a_ref) | copy-start | bytes 786436
  15.1 23.8 %collective-permute-start.5 = (bf16[256,512]{1,0:T(8,128)(2,1)S(1)}, bf16[256,512]{1,0:T(8,128)(2,1)S(1)}, u32[]{:S(2)}, u32[]{:S(2)}) collective-permute-start(bf16[256,512]{1,0:T(8,128)(2,1)S(1)} %collective-permute-done.4.a_ref), channel_id=1, source_target_pairs={{0,1},{1,0},{2,3},{3,2},{4,5},{5,4},{6,7},{7,6},{8,9},{9,8},{10,11... | collective-permute-start | bytes 786440 | tf_op jit(solution)/shard_map/ppermute | solution.py:30
  25.3 13.6 %copy-start.6 = (bf16[256,512]{1,0:T(8,128)(2,1)}, bf16[256,512]{1,0:T(8,128)(2,1)S(1)}, u32[]{:S(2)}) copy-start(bf16[256,512]{1,0:T(8,128)(2,1)S(1)} %collective-permute-done.2.a_ref) | copy-start | bytes 786436
  25.3 26.8 %collective-permute-start.3 = (bf16[256,512]{1,0:T(8,128)(2,1)S(1)}, bf16[256,512]{1,0:T(8,128)(2,1)S(1)}, u32[]{:S(2)}, u32[]{:S(2)}) collective-permute-start(bf16[256,512]{1,0:T(8,128)(2,1)S(1)} %collective-permute-done.2.a_ref), channel_id=1, source_target_pairs={{0,1},{1,0},{2,3},{3,2},{4,5},{5,4},{6,7},{7,6},{8,9},{9,8},{10,11... | collective-permute-start | bytes 786440 | tf_op jit(solution)/shard_map/ppermute | solution.py:30
  25.3 13.6 %copy-start.5 = (bf16[256,512]{1,0:T(8,128)(2,1)}, bf16[256,512]{1,0:T(8,128)(2,1)S(1)}, u32[]{:S(2)}) copy-start(bf16[256,512]{1,0:T(8,128)(2,1)S(1)} %collective-permute-done.a_ref) | copy-start | bytes 786436
  25.3 40.0 %collective-permute-start.1 = (bf16[256,512]{1,0:T(8,128)(2,1)S(1)}, bf16[256,512]{1,0:T(8,128)(2,1)S(1)}, u32[]{:S(2)}, u32[]{:S(2)}) collective-permute-start(bf16[256,512]{1,0:T(8,128)(2,1)S(1)} %collective-permute-done.a_ref), channel_id=1, source_target_pairs={{0,1},{1,0},{2,3},{3,2},{4,5},{5,4},{6,7},{7,6},{8,9},{9,8},{10,11... | collective-permute-start | bytes 786440 | tf_op jit(solution)/shard_map/ppermute | solution.py:30
  78.5 5.5 %collective-permute-start.9 = (f32[8,8,256]{2,1,0:T(8,128)}, f32[8,8,256]{2,1,0:T(8,128)S(1)}, u32[]{:S(2)}, u32[]{:S(2)}) collective-permute-start(f32[8,8,256]{2,1,0:T(8,128)} %get-tuple-element.37), channel_id=1, source_target_pairs={{0,24},{8,16},{16,8},{24,0},{1,25},{9,17},{17,9},{25,1},{2,26},{10... | collective-permute-start | bytes 196616 | tf_op jit(solution)/shard_map/ppermute | solution.py:30
  81.0 4.5 %collective-permute-start.8 = (f32[8,8,256]{2,1,0:T(8,128)}, f32[8,8,256]{2,1,0:T(8,128)S(1)}, u32[]{:S(2)}, u32[]{:S(2)}) collective-permute-start(f32[8,8,256]{2,1,0:T(8,128)} %get-tuple-element.37), channel_id=1, source_target_pairs={{0,16},{8,24},{16,0},{24,8},{1,17},{9,25},{17,1},{25,9},{2,18},{10... | collective-permute-start | bytes 196616 | tf_op jit(solution)/shard_map/ppermute | solution.py:30
  81.5 4.5 %collective-permute-start.7 = (f32[8,8,256]{2,1,0:T(8,128)}, f32[8,8,256]{2,1,0:T(8,128)S(1)}, u32[]{:S(2)}, u32[]{:S(2)}) collective-permute-start(f32[8,8,256]{2,1,0:T(8,128)} %get-tuple-element.37), channel_id=1, source_target_pairs={{0,8},{8,0},{16,24},{24,16},{1,9},{9,1},{17,25},{25,17},{2,10},{10... | collective-permute-start | bytes 196616 | tf_op jit(solution)/shard_map/ppermute | solution.py:30
  104.3 20.5 %all-to-all-start.3 = ((bf16[4,160,1024]{2,1,0:T(8,128)(2,1)}), bf16[4,160,1024]{2,1,0:T(8,128)(2,1)S(1)}, u32[]{:S(2)}, u32[]{:S(2)}) async-start(bf16[4,160,1024]{2,1,0:T(8,128)(2,1)} %ups.7), calls=%async_computation.3 | async-start | bytes 2621440 | tf_op jit(solution)/shard_map/all_to_all | solution.py:316
  124.9 31.6 %all-to-all-start.2 = ((bf16[4,160,1024]{2,1,0:T(8,128)(2,1)}), bf16[4,160,1024]{2,1,0:T(8,128)(2,1)S(1)}, u32[]{:S(2)}, u32[]{:S(2)}) async-start(bf16[4,160,1024]{2,1,0:T(8,128)(2,1)} %ups.6), calls=%async_computation.2 | async-start | bytes 2621440 | tf_op jit(solution)/shard_map/all_to_all | solution.py:316
  156.4 25.6 %all-to-all-start = ((bf16[4,160,1024]{2,1,0:T(8,128)(2,1)}), bf16[4,160,1024]{2,1,0:T(8,128)(2,1)}, u32[]{:S(2)}, u32[]{:S(2)}) async-start(bf16[4,160,1024]{2,1,0:T(8,128)(2,1)} %ups.4), calls=%async_computation | async-start | bytes 2621440 | tf_op jit(solution)/shard_map/all_to_all | solution.py:316
  175.4 29.7 %collective-permute-start.10 = (bf16[4,256,512]{2,1,0:T(8,128)(2,1)}, bf16[4,256,512]{2,1,0:T(8,128)(2,1)}, u32[]{:S(2)}, u32[]{:S(2)}) collective-permute-start(bf16[4,256,512]{2,1,0:T(8,128)(2,1)} %get-tuple-element.63), channel_id=1, source_target_pairs={{0,1},{1,0},{2,3},{3,2},{4,5},{5,4},{6,7},{7,6},{8,9},{9,8},{10,11... | collective-permute-start | bytes 3145736 | tf_op jit(solution)/shard_map/ppermute | solution.py:30
  182.0 21.3 %all-to-all-start.1 = ((bf16[4,160,1024]{2,1,0:T(8,128)(2,1)}), bf16[4,160,1024]{2,1,0:T(8,128)(2,1)S(1)}, u32[]{:S(2)}, u32[]{:S(2)}) async-start(bf16[4,160,1024]{2,1,0:T(8,128)(2,1)} %ups.5), calls=%async_computation.1 | async-start | bytes 2621440 | tf_op jit(solution)/shard_map/all_to_all | solution.py:316
  186.4 1.9 copy-start
  189.0 16.0 %copy-start.1 = (f32[160,1024]{1,0:T(8,128)S(1)}, f32[160,1024]{1,0:T(8,128)}, u32[]{:S(2)}) copy-start(f32[160,1024]{1,0:T(8,128)} %copy-done) | copy-start | bytes 1966084
  205.0 1.2 copy-start.2
  207.9 11.1 %collective-permute-start.11 = (bf16[256,512]{1,0:T(8,128)(2,1)S(1)}, bf16[256,512]{1,0:T(8,128)(2,1)S(1)}, u32[]{:S(2)}, u32[]{:S(2)}) collective-permute-start(bf16[256,512]{1,0:T(8,128)(2,1)S(1)} %get-tuple-element.66), channel_id=1, source_target_pairs={{0,2},{1,3},{2,0},{3,1},{4,6},{5,7},{6,4},{7,5},{8,10},{9,11},{10,... | collective-permute-start | bytes 786440 | tf_op jit(solution)/shard_map/ppermute | solution.py:30
  212.2 15.4 %collective-permute-start.13 = (bf16[256,512]{1,0:T(8,128)(2,1)S(1)}, bf16[256,512]{1,0:T(8,128)(2,1)S(1)}, u32[]{:S(2)}, u32[]{:S(2)}) collective-permute-start(bf16[256,512]{1,0:T(8,128)(2,1)S(1)} %get-tuple-element.67), channel_id=1, source_target_pairs={{0,6},{1,7},{2,4},{3,5},{4,2},{5,3},{6,0},{7,1},{8,14},{9,15},{10,... | collective-permute-start | bytes 786440 | tf_op jit(solution)/shard_map/ppermute | solution.py:30
  214.7 21.5 %collective-permute-start.12 = (bf16[256,512]{1,0:T(8,128)(2,1)S(1)}, bf16[256,512]{1,0:T(8,128)(2,1)S(1)}, u32[]{:S(2)}, u32[]{:S(2)}) collective-permute-start(bf16[256,512]{1,0:T(8,128)(2,1)S(1)} %get-tuple-element.68), channel_id=1, source_target_pairs={{0,4},{1,5},{2,6},{3,7},{4,0},{5,1},{6,2},{7,3},{8,12},{9,13},{10,... | collective-permute-start | bytes 786440 | tf_op jit(solution)/shard_map/ppermute | solution.py:30
  (6 other events, 4.6 us)

commit v2 on v1

v2 whole, which is shorter than its diff:
```python
import functools
import math

import jax
import jax.numpy as jnp
from jax import lax
from jax.experimental import pallas as pl
from jax.experimental.pallas import tpu as pltpu
from jax.sharding import PartitionSpec as P

HD = 128
PAIR = 2
WIDE = 4
VMEM = 60 << 20
NT = (((1,), (1,)), ((), ()))
TN = (((0,), (0,)), ((), ()))
NN = (((1,), (0,)), ((), ()))
SCALE = 1.0 / math.sqrt(HD)
LOG2E = math.log2(math.e)
F32 = jnp.float32
BF16 = jnp.bfloat16


def dot(a, b, dims=NN):
    return lax.dot_general(a, b, dims, preferred_element_type=F32)


def swap(array, axis, distance):
    count = lax.axis_size(axis)
    return lax.ppermute(array, axis, [(i, i ^ distance) for i in range(count)])


def masked(s, gap):
    rows = lax.broadcasted_iota(jnp.int32, s.shape, 0)
    cols = lax.broadcasted_iota(jnp.int32, s.shape, 1)
    return jnp.where(rows - cols > gap, -jnp.inf, s)


def lanes(head):
    return slice(head * HD, (head + 1) * HD)


def join(parts):
    m = functools.reduce(jnp.maximum, [p[0] for p in parts])
    factors = [jnp.exp2(p[0] - m) for p in parts]
    t = sum(p[1] * f for p, f in zip(parts, factors))
    d = sum(p[2] * f for p, f in zip(parts, factors))
    return m, t, d


def triple(ref, head):
    return tuple(ref[3 * head + i : 3 * head + i + 1, :] for i in range(3))


def stats_kernel(first, pieces, gaps_ref, uk_ref, uv_ref, q_ref, do_ref, *refs):
    lat_refs = refs[:pieces]
    k2_ref, v_ref, st_ref = refs[-3:]
    rb = lat_refs[0].shape[0]
    qn = q_ref.shape[0]
    step_heads = range(q_ref.shape[1] // HD)
    weights = [jnp.concatenate([uk_ref[:, lanes(a)], uv_ref[:, lanes(a)]], axis=1) for a in step_heads]
    q = [q_ref[:, lanes(a)] for a in step_heads]
    qq = [jnp.concatenate([x, x], axis=1) for x in q]
    do = [do_ref[:, lanes(a)] for a in step_heads]
    parts = [[] if first == 0 else [triple(refs[pieces].at[a // PAIR], a % PAIR)] for a in step_heads]
    for a in step_heads:
        for i, lat_ref in enumerate(lat_refs):
            rows = pl.ds(i * rb, rb)
            kv = dot(lat_ref[...], weights[a])
            k = kv[:, :HD] * (SCALE * LOG2E)
            hi = k.astype(BF16)
            lo = (k - hi.astype(F32)).astype(BF16)
            k2 = jnp.concatenate([hi, lo], axis=1)
            v = kv[:, HD:].astype(BF16)
            k2_ref[a, rows, :] = k2
            v_ref[a, rows, :] = v
            s = masked(dot(k2, qq[a], NT), gaps_ref[first + i])
            gp = dot(v, do[a], NT)
            m = jnp.maximum(jnp.max(s, axis=0, keepdims=True), -1e30)
            w = jnp.exp2(s - m)
            parts[a].append((m, jnp.sum(w, axis=0, keepdims=True), jnp.sum(w * gp, axis=0, keepdims=True)))
    pad = jnp.zeros((8 - 3 * PAIR, qn), F32)
    for j in range(len(step_heads) // PAIR):
        own = [x for a in range(j * PAIR, (j + 1) * PAIR) for x in join(parts[a])]
        st_ref[j] = jnp.concatenate(own + [pad], axis=0)


def run_stats(first, gaps, pieces, up_key, up_value, queries, grad_out, before):
    rb, depth = pieces[0].shape
    rows = rb * len(pieces)
    heads = queries.shape[1] // HD
    qn = queries.shape[0]
    wide = WIDE * HD
    col = lambda g, *_: (0, g)
    whole = pl.BlockSpec((rb, depth), lambda g, *_: (0, 0))
    st_spec = pl.BlockSpec((WIDE // PAIR, 8, qn), lambda g, *_: (g, 0, 0))
    extra = () if before is None else (before,)
    return pl.pallas_call(
        functools.partial(stats_kernel, first, len(pieces)),
        out_shape=(
            jax.ShapeDtypeStruct((heads, rows, 2 * HD), BF16),
            jax.ShapeDtypeStruct((heads, rows, HD), BF16),
            jax.ShapeDtypeStruct((heads // PAIR, 8, qn), F32),
        ),
        grid_spec=pltpu.PrefetchScalarGridSpec(
            num_scalar_prefetch=1,
            grid=(heads // WIDE,),
            in_specs=[
                pl.BlockSpec((depth, wide), col),
                pl.BlockSpec((depth, wide), col),
                pl.BlockSpec((qn, wide), col),
                pl.BlockSpec((qn, wide), col),
            ]
            + [whole] * len(pieces)
            + [st_spec] * len(extra),
            out_specs=[
                pl.BlockSpec((WIDE, rows, 2 * HD), lambda g, *_: (g, 0, 0)),
                pl.BlockSpec((WIDE, rows, HD), lambda g, *_: (g, 0, 0)),
                st_spec,
            ],
        ),
        compiler_params=pltpu.CompilerParams(vmem_limit_bytes=VMEM),
        cost_estimate=pl.CostEstimate(
            flops=heads * rows * HD * 8 * depth, bytes_accessed=heads * rows * HD * 6, transcendentals=0
        ),
        name="stats",
    )(gaps, up_key, up_value, queries, grad_out, *pieces, *extra)


def head_grads(gaps_ref, q_ref, do_ref, st_refs, blocks, gk_ref, gv_ref):
    qn = q_ref.shape[0]
    pair = range(PAIR)
    q = [q_ref[:, lanes(a)] for a in pair]
    qq = [jnp.concatenate([x, x], axis=1) for x in q]
    do = [do_ref[:, lanes(a)] for a in pair]
    shift, delta = [], []
    for a in pair:
        m, t, d = join([triple(ref, a) for ref in st_refs])
        shift.append(m + jnp.log2(t))
        delta.append(d / t)
    gq = [jnp.zeros((qn, 2 * HD), F32) for a in pair]
    base = 0
    for chunk, k2_ref, v_ref, lower, size in blocks:
        rb = size // 2
        here, rows = pl.ds(lower, size), pl.ds(base, size)
        for a in pair:
            k2 = k2_ref[a, here, :]
            s = dot(k2, qq[a], NT)
            s = jnp.concatenate(
                [masked(s[:rb], gaps_ref[2 * chunk]), masked(s[rb:], gaps_ref[2 * chunk + 1])], axis=0
            )
            gp = dot(v_ref[a, here, :], do[a], NT)
            p = jnp.exp2(s - shift[a])
            ds = (p * (gp - delta[a]) * SCALE).astype(BF16)
            low = p.astype(BF16)
            gk_ref[rows, lanes(a)] = dot(ds, q[a]).astype(BF16)
            gv_ref[rows, lanes(a)] = dot(low, do[a]).astype(BF16)
            gq[a] = gq[a] + dot(ds, k2, TN)
        base += size
    return jnp.concatenate([(x[:, :HD] + x[:, HD:]) * (1.0 / (SCALE * LOG2E)) for x in gq], axis=1)


def up_grads(step, terms, gq, out_ref):
    qn, wide = gq.shape
    n = out_ref.shape[0]
    qb = qn // n
    half = out_ref.shape[2] // 2
    for side in range(2):
        gu = sum(dot(latt, sides[side]) for latt, sides in terms)
        ub = gu.shape[0] // n
        cols = pl.ds(pl.multiple_of(side * half + step * wide, wide), wide)
        for r in range(n):
            lower = r * qb + side * (qb // 2)
            out_ref[r, 0:ub, cols] = gu[r * ub : (r + 1) * ub].astype(BF16)
            out_ref[r, ub:, cols] = gq[lower : lower + qb // 2].astype(BF16)


def whole_kernel(n, held, gaps_ref, q_ref, do_ref, *refs):
    st_refs, refs = refs[:n], refs[n:]
    refs = refs[:5] + refs[5 + held :]
    ka_ref, kb_ref, va_ref, vb_ref, latt_ref, gk_ref, gv_ref, out_ref = refs
    size = ka_ref.shape[1]
    blocks = [(1 + i, kb_ref, vb_ref, i * size, size) for i in range(kb_ref.shape[1] // size)]
    blocks.append((0, ka_ref, va_ref, 0, size))
    gq = head_grads(gaps_ref, q_ref, do_ref, st_refs, blocks, gk_ref, gv_ref)
    terms = [(latt_ref[...], (gk_ref[...], gv_ref[...]))]
    up_grads(pl.program_id(0), terms, gq, out_ref)


def add_latent(gl_ref, own, other):
    total = gl_ref[...]
    for gk, gv, uk, uv in [own, other] if own else [other]:
        total = total + dot(gk[...], uk[...], NT) + dot(gv[...], uv[...], NT)
    gl_ref[...] = total


def put_latent(gl_ref, keep_ref, send_ref):
    steps, rb, _ = keep_ref.shape
    for i in range(steps):
        keep_ref[i] = gl_ref[2 * i * rb : (2 * i + 1) * rb, :].astype(BF16)
        send_ref[i] = gl_ref[(2 * i + 1) * rb : (2 * i + 2) * rb, :].astype(BF16)


def far_kernel(n, chunks, own, gaps_ref, q_ref, do_ref, *refs):
    st_refs, refs = refs[:n], refs[n:]
    k_refs, v_refs, refs = refs[: len(chunks)], refs[len(chunks) : 2 * len(chunks)], refs[2 * len(chunks) :]
    uk_ref, uv_ref, uk2_ref, uv2_ref, ok_ref, ov_ref, gk_ref, gv_ref, gq_ref, keep_ref, send_ref, gl_ref = refs
    step = pl.program_id(0)

    @pl.when(step == 0)
    def _():
        gl_ref[...] = jnp.zeros_like(gl_ref)

    @pl.when(step < own)
    def _():
        blocks = [(c, k, v, 0, k.shape[1]) for c, k, v in zip(chunks, k_refs, v_refs)]
        gq_ref[...] = head_grads(gaps_ref, q_ref, do_ref, st_refs, blocks, gk_ref, gv_ref)
        add_latent(gl_ref, (gk_ref, gv_ref, uk_ref, uv_ref), (ok_ref, ov_ref, uk2_ref, uv2_ref))

    @pl.when(step >= own)
    def _():
        add_latent(gl_ref, None, (ok_ref, ov_ref, uk2_ref, uv2_ref))

    @pl.when(step == pl.num_programs(0) - 1)
    def _():
        put_latent(gl_ref, keep_ref, send_ref)


def near_kernel(n, chunks, own, gaps_ref, q_ref, do_ref, *refs):
    st_refs, refs = refs[:n], refs[n:]
    k_refs, v_refs, refs = refs[: len(chunks)], refs[len(chunks) : 2 * len(chunks)], refs[2 * len(chunks) :]
    uk_ref, uv_ref, uk2_ref, uv2_ref, ok_ref, ov_ref, latt_ref, fk_ref, fv_ref, fq_ref = refs[:10]
    out_ref, keep_ref, send_ref, gk_ref, gv_ref, gl_ref = refs[10:]
    step = pl.program_id(0)

    @pl.when(step == 0)
    def _():
        gl_ref[...] = jnp.zeros_like(gl_ref)

    @pl.when(step < own)
    def _():
        blocks = [(c, k, v, 0, k.shape[1]) for c, k, v in zip(chunks, k_refs, v_refs)]
        gq = fq_ref[...] + head_grads(gaps_ref, q_ref, do_ref, st_refs, blocks, gk_ref, gv_ref)
        rest = fk_ref.shape[0]
        terms = [
            (latt_ref[:, :rest], (fk_ref[...], fv_ref[...])),
            (latt_ref[:, rest:], (gk_ref[...], gv_ref[...])),
        ]
        up_grads(step, terms, gq, out_ref)
        add_latent(gl_ref, (gk_ref, gv_ref, uk_ref, uv_ref), (ok_ref, ov_ref, uk2_ref, uv2_ref))

    @pl.when(step >= own)
    def _():
        add_latent(gl_ref, None, (ok_ref, ov_ref, uk2_ref, uv2_ref))

    @pl.when(step == pl.num_programs(0) - 1)
    def _():
        put_latent(gl_ref, keep_ref, send_ref)


def turn_kernel(*refs):
    rb = refs[0].shape[0]
    for i, ref in enumerate(refs[:-1]):
        refs[-1][:, i * rb : (i + 1) * rb] = ref[...].T


def run_turn(pieces):
    rb, depth = pieces[0].shape
    return pl.pallas_call(
        turn_kernel,
        out_shape=jax.ShapeDtypeStruct((depth, rb * len(pieces)), BF16),
        compiler_params=pltpu.CompilerParams(vmem_limit_bytes=VMEM),
        name="turn",
    )(*pieces)


def part_shape(n, depth, qn, cols):
    return jax.ShapeDtypeStruct((n, depth // n + qn // n // 2, 2 * cols), BF16)


def run_whole(gaps, queries, grad_out, stats, k2, v, latt, lower, upper, pairs, held=()):
    n = len(stats)
    depth = latt.shape[0]
    rows = sum(x.shape[1] for x in k2)
    qn = queries.shape[0]
    wide = PAIR * HD
    cols = (upper - lower) * wide
    col = lambda g, *_: (0, lower + g)
    block = lambda g, *_: (lower + g, 0, 0)
    part = part_shape(n, depth, qn, cols)
    operands = (gaps, queries, grad_out, *stats, *k2, *v, latt)
    return pl.pallas_call(
        functools.partial(whole_kernel, n, len(held)),
        out_shape=(jax.ShapeDtypeStruct((rows, pairs * wide), BF16),) * 2 + (part,),
        grid_spec=pltpu.PrefetchScalarGridSpec(
            num_scalar_prefetch=1,
            grid=(upper - lower,),
            in_specs=[pl.BlockSpec((qn, wide), col)] * 2
            + [pl.BlockSpec((None, 8, qn), block)] * n
            + [pl.BlockSpec((PAIR, *x.shape[1:]), block) for x in (*k2, *v)]
            + [pl.BlockSpec(latt.shape, lambda g, *_: (0, 0))]
            + [pl.BlockSpec(memory_space=pl.ANY)] * len(held),
            out_specs=[pl.BlockSpec((rows, wide), col)] * 2
            + [pl.BlockSpec(part.shape, lambda g, *_: (0, 0, 0))],
        ),
        input_output_aliases={len(operands) + i: i for i in range(len(held))},
        compiler_params=pltpu.CompilerParams(vmem_limit_bytes=VMEM),
        cost_estimate=pl.CostEstimate(
            flops=cols * rows * 2 * (7 * qn + 2 * depth), bytes_accessed=cols * rows * 10, transcendentals=0
        ),
        name="whole",
    )(*operands, *held)


def run_split(far, gaps, queries, grad_out, stats, k2, v, chunks, up_key, up_value, other, first, pairs,
              latt=None, before=()):
    n = len(stats)
    size = k2[0].shape[1]
    depth = up_key.shape[0]
    rb = size // 2
    rows = size * len(chunks)
    qn = queries.shape[0]
    wide = PAIR * HD
    cols = pairs * wide
    last = pairs - 1
    own = lambda g, *_: (0, first + jnp.minimum(g, last))
    own3 = lambda g, *_: (first + jnp.minimum(g, last), 0, 0)
    out = lambda g, *_: (0, jnp.minimum(g, last))
    col = lambda g, *_: (0, g)
    fixed = lambda g, *_: (0, 0)
    fixed3 = lambda g, *_: (0, 0, 0)

    def rows_of(chunk):
        if chunk == 0:
            return 0, own3
        return 1, lambda g, *_: (first + jnp.minimum(g, last), chunk - 1, 0)

    picked = [rows_of(c) for c in chunks]
    in_specs = [pl.BlockSpec((qn, wide), own)] * 2 + [pl.BlockSpec((None, 8, qn), own3)] * n
    in_specs += [pl.BlockSpec((PAIR, size, 2 * HD), index) for _, index in picked]
    in_specs += [pl.BlockSpec((PAIR, size, HD), index) for _, index in picked]
    in_specs += [pl.BlockSpec((depth, wide), own)] * 2 + [pl.BlockSpec((depth, wide), col)] * 2
    in_specs += [pl.BlockSpec((rows, wide), lambda g, *_: (0 if far else other[0].shape[0] // rows - 1, g))] * 2
    grads = (jax.ShapeDtypeStruct((rows, cols), BF16),) * 2
    sums = (jax.ShapeDtypeStruct((len(chunks), rb, depth), BF16),) * 2
    sum_specs = [pl.BlockSpec(sums[0].shape, fixed3)] * 2
    gl = pltpu.VMEM((rows, depth), F32)
    if far:
        kernel = far_kernel
        out_shape = grads + (jax.ShapeDtypeStruct((qn, cols), F32),) + sums
        out_specs = [pl.BlockSpec((rows, wide), out)] * 2 + [pl.BlockSpec((qn, wide), out)] + sum_specs
        scratch = [gl]
    else:
        kernel = near_kernel
        part = part_shape(n, depth, qn, cols)
        in_specs += [pl.BlockSpec(latt.shape, fixed)]
        in_specs += [pl.BlockSpec((before[0].shape[0], wide), out)] * 2 + [pl.BlockSpec((qn, wide), out)]
        out_shape = (part,) + sums
        out_specs = [pl.BlockSpec(part.shape, fixed3)] + sum_specs
        scratch = [pltpu.VMEM((rows, wide), BF16)] * 2
        scratch += [gl]
    return pl.pallas_call(
        functools.partial(kernel, n, chunks, pairs),
        out_shape=out_shape,
        grid_spec=pltpu.PrefetchScalarGridSpec(
            num_scalar_prefetch=1,
            grid=(first,),
            in_specs=in_specs,
            out_specs=out_specs,
            scratch_shapes=scratch,
        ),
        compiler_params=pltpu.CompilerParams(vmem_limit_bytes=VMEM),
        cost_estimate=pl.CostEstimate(
            flops=cols * rows * 2 * (7 * qn + 4 * depth) + first * wide * rows * 4 * depth,
            bytes_accessed=cols * rows * 10,
            transcendentals=0,
        ),
        name="far" if far else "near",
    )(gaps, queries, grad_out, *stats, *[k2[i] for i, _ in picked], *[v[i] for i, _ in picked],
      up_key, up_value, up_key, up_value, *other, *([] if far else [latt]), *before)


def after(value, *others):
    return lax.optimization_barrier((value, *others))[0]


def local(queries, grad_out, latent, up_key, up_value):
    heads = queries.shape[1] // HD
    qn = queries.shape[0]
    n = lax.axis_size("ctx")
    mates = lax.axis_size("head")
    rb, depth = latent.shape
    chunks = mates // 2
    near = 1

    firsts = [latent] + [swap(latent, "head", 2 * k) for k in range(1, chunks)]
    starts = (lax.axis_index("ctx") * mates + (lax.axis_index("head") ^ jnp.arange(mates))) * rb
    gaps = (rb * mates * n - qn - starts).astype(jnp.int32)
    k2, v, every, stats = [], [], [], None
    for which in ([0], list(range(1, chunks))):
        pieces = []
        for c in which:
            mine = firsts[c] if stats is None else after(firsts[c], stats)
            pieces += [mine, swap(mine, "head", 1)]
        one_k2, one_v, stats = run_stats(
            2 * which[0], gaps, pieces, up_key, up_value, queries, grad_out, stats
        )
        k2.append(one_k2)
        v.append(one_v)
        every += pieces
    latt = run_turn([after(every[2], stats)] + every[3:] + every[:2])
    stats = [stats] + [swap(stats, "ctx", k) for k in range(1, n)]

    pairs = heads // PAIR
    first = 3 * pairs // 4
    half = first // 3
    held, outs = (), []
    for lower, upper in ((0, half), (half, first)):
        gk, gv, part = run_whole(gaps, queries, grad_out, stats, k2, v, latt, lower, upper, first, held)
        held = (gk, gv)
        outs.append(lax.all_to_all(part, "ctx", 0, 0, tiled=True))
    split = functools.partial(run_split, up_key=up_key, up_value=up_value, other=(gk, gv), first=first,
                              pairs=pairs - first, queries=queries, grad_out=grad_out, stats=stats, k2=k2, v=v)
    fk, fv, fq, far, far_away = split(True, after(gaps, outs[0]), chunks=list(range(near, chunks)))
    far = far.astype(F32) + swap(far_away, "head", 1).astype(F32)
    far = far.astype(BF16)
    part, close, close_away = split(
        False, after(gaps, far), chunks=list(range(near)), latt=latt, before=(fk, fv, fq)
    )
    outs.append(lax.all_to_all(after(part, outs[1]), "ctx", 0, 0, tiled=True))
    got = [swap(far[k], "head", 2 * (near + k)) for k in range(chunks - near)]
    close = close.astype(F32) + swap(after(close_away, *got), "head", 1).astype(F32)
    grad_latent = close[0]
    for x in got:
        grad_latent = grad_latent + x.astype(F32)

    sums = [jnp.sum(o.astype(F32), axis=0) for o in outs]
    ub = depth // n
    grad_key = jnp.concatenate([s[:ub, : s.shape[1] // 2] for s in sums], axis=1)
    grad_value = jnp.concatenate([s[:ub, s.shape[1] // 2 :] for s in sums], axis=1)
    grad_q = jnp.concatenate(
        [jnp.concatenate([s[ub:, : s.shape[1] // 2], s[ub:, s.shape[1] // 2 :]], axis=0) for s in sums], axis=1
    )
    return (grad_q, grad_latent, grad_key, grad_value)


def solution(mesh):
    return jax.shard_map(
        local,
        mesh=mesh,
        in_specs=(
            P(None, "head"),
            P(None, "head"),
            P(("ctx", "head"), None),
            P(None, "head"),
            P(None, "head"),
        ),
        out_specs=(P("ctx", "head"), P(("ctx", "head"), None), P("ctx", "head"), P("ctx", "head")),
        check_vma=False,
    )
```

time: 239 us -> 172 us (0.72)
  the two profiles are of different devices: /device:TPU:0 before, /device:TPU:17 now
where the time goes in v2:
time: 172 us; the launch traced here: 169 us
  Pallas kernels  103 us (60%)
  waiting for transfers between devices  26.7 us (16%)
  starting transfers between devices  25.6 us (15%)
  other arithmetic  8.9 us (5%)
  local copies, waits for them, and re-layouts  4.72 us (3%)
    pallas_call x2, Pallas kernels, run_whole(): pl.pallas_call(functools.partial(whole_kernel, n, len(held)), out_shape=(...  36.6 us
    pallas_call x2, Pallas kernels, run_split(): pl.pallas_call(functools.partial(kernel, n, chunks, pairs), out_shape=out...  33.1 us
    pallas_call x2, Pallas kernels, run_stats(): pl.pallas_call(functools.partial(stats_kernel, first, len(pieces)), out_s...  29.5 us
    ppermute x15, waiting for transfers between devices, swap(): return lax.ppermute(array, axis, [(i, i ^ distance) for i in range(count)])  15.8 us
    ppermute x15, starting transfers between devices, swap(): return lax.ppermute(array, axis, [(i, i ^ distance) for i in range(count)])  13.9 us
    all_to_all x1, waiting for transfers between devices, local(): outs.append(lax.all_to_all(after(part, outs[1]), 'ctx', 0, 0, tiled=True))  10.9 us
    all_to_all x2, starting transfers between devices, local(): outs.append(lax.all_to_all(part, 'ctx', 0, 0, tiled=True))  7.38 us
    all_to_all x1, starting transfers between devices, local(): outs.append(lax.all_to_all(after(part, outs[1]), 'ctx', 0, 0, tiled=True))  4.33 us
  transfers between devices with their start and end apart: 18, of which 8 were waited for; matrix products, arithmetic and copies ran while one was open for 4% of the time, Pallas kernels for 41%

profile of v2, /device:TPU:17, one launch (start us, length us, event | category | flops | bytes accessed | tf_op | source)
XLA Modules:
  0.0 169.4 jit_solution(6654267009208016578)
XLA Ops:
  1.4 1.4 collective-permute-start
  2.7 1.3 collective-permute-start.5
  5.3 9.7 %stats.2 = (bf16[16,512,256]{2,1,0:T(8,128)(2,1)}, bf16[16,512,128]{2,1,0:T(8,128)(2,1)}, f32[8,8,256]{2,1,0:T(8,128)}) custom-call(s32[8]{0:T(128)} %multiply_subtract_fusion.gaps_ref, bf16[512,2048]{1,0:T(8,128)(2,1)} %refs_8_.1, bf16[512,2048]{1,0:T(8,128)(2,1)} %refs_9_.1, bf16[256,2048]{1,0:T(8,128)(2,1)} %q_ref.11, bf16[256,2048]{1,0:T(8,128)(2,1)} %do_ref.11, ...), custom_call_target="tpu_custom_call" | custom-call | flops 4294967296 | bytes 6291456 | tf_op jit(solution)/shard_map/stats/pallas_call | solution.py:98
  15.0 12.6 %collective-permute-done.5.refs_4_ = bf16[256,512]{1,0:T(8,128)(2,1)S(1)} collective-permute-done((bf16[256,512]{1,0:T(8,128)(2,1)}, bf16[256,512]{1,0:T(8,128)(2,1)S(1)}, u32[]{:S(2)}, u32[]{:S(2)}) %collective-permute-start.5) | collective-permute-done | bytes 262176 | tf_op jit(solution)/shard_map/ppermute | solution.py:30
  31.1 19.8 %stats.3 = (bf16[16,1536,256]{2,1,0:T(8,128)(2,1)}, bf16[16,1536,128]{2,1,0:T(8,128)(2,1)}, f32[8,8,256]{2,1,0:T(8,128)}) custom-call(s32[8]{0:T(128)} %multiply_subtract_fusion.gaps_ref, bf16[512,2048]{1,0:T(8,128)(2,1)} %refs_8_.1, bf16[512,2048]{1,0:T(8,128)(2,1)} %refs_9_.1, bf16[256,2048]{1,0:T(8,128)(2,1)} %q_ref.11, bf16[256,2048]{1,0:T(8,128)(2,1)} %do_ref.11, ...), custom_call_target="tpu_custom_call" | custom-call | flops 12884901888 | bytes 18874368 | tf_op jit(solution)/shard_map/stats/pallas_call | solution.py:98
  50.9 2.2 %collective-permute-start.9 = (f32[8,8,256]{2,1,0:T(8,128)}, f32[8,8,256]{2,1,0:T(8,128)S(1)}, u32[]{:S(2)}, u32[]{:S(2)}) collective-permute-start(f32[8,8,256]{2,1,0:T(8,128)} %get-tuple-element.36.refs_0_), channel_id=1, source_target_pairs={{0,24},{8,16},{16,8},{24,0},{1,25},{9,17},{17,9},{25,1},{2,26},{10... | collective-permute-start | bytes 196616 | tf_op jit(solution)/shard_map/ppermute | solution.py:30
  53.6 3.5 %turn.1.refs_8_.refs_12_ = bf16[512,2048]{1,0:T(8,128)(2,1)} custom-call(bf16[256,512]{1,0:T(8,128)(2,1)} %copy-done.7, bf16[256,512]{1,0:T(8,128)(2,1)} %copy-done.10, bf16[256,512]{1,0:T(8,128)(2,1)} %copy-done.6, bf16[256,512]{1,0:T(8,128)(2,1)} %copy-done.11, bf16[256,512]{1,0:T(8,128)(2,1)} %copy-done.8, bf16[256,512]{1,0:T(8,128)(2,1)} %copy-done.12, ...), custom_call_target="tpu_custom_call" | custom-call | tf_op jit(solution)/shard_map/turn/pallas_call | solution.py:269
  57.8 13.6 %whole.2 = (bf16[2048,1536]{1,0:T(8,128)(2,1)}, bf16[2048,1536]{1,0:T(8,128)(2,1)}, bf16[4,160,1024]{2,1,0:T(8,128)(2,1)}) custom-call(s32[8]{0:T(128)} %multiply_subtract_fusion.gaps_ref, bf16[256,2048]{1,0:T(8,128)(2,1)} %q_ref.11, bf16[256,2048]{1,0:T(8,128)(2,1)} %do_ref.11, f32[8,8,256]{2,1,0:T(8,128)} %get-tuple-element.36.refs_0_, ...), custom_call_target="tpu_custom_call" | custom-call | flops 5905580032 | bytes 10485760 | tf_op jit(solution)/shard_map/whole/pallas_call | solution.py:292
  71.4 3.7 %all-to-all-start = ((bf16[4,160,1024]{2,1,0:T(8,128)(2,1)}), bf16[4,160,1024]{2,1,0:T(8,128)(2,1)S(1)}, u32[]{:S(2)}, u32[]{:S(2)}) async-start(bf16[4,160,1024]{2,1,0:T(8,128)(2,1)} %get-tuple-element.42), calls=%async_computation | async-start | bytes 2621440 | tf_op jit(solution)/shard_map/all_to_all | solution.py:421
  75.2 22.9 %whole.3 = (bf16[2048,1536]{1,0:T(8,128)(2,1)}, bf16[2048,1536]{1,0:T(8,128)(2,1)}, bf16[4,160,2048]{2,1,0:T(8,128)(2,1)}) custom-call(s32[8]{0:T(128)} %multiply_subtract_fusion.gaps_ref, bf16[256,2048]{1,0:T(8,128)(2,1)} %q_ref.11, bf16[256,2048]{1,0:T(8,128)(2,1)} %do_ref.11, ...), custom_call_target="tpu_custom_call", output_to_operand_aliasing={{0}: (12, {}), {1}: (13, {})} | custom-call | flops 11811160064 | bytes 20971520 | tf_op jit(solution)/shard_map/whole/pallas_call | solution.py:292
  98.1 1.1 copy-done
  99.2 3.7 %all-to-all-start.1 = ((bf16[4,160,2048]{2,1,0:T(8,128)(2,1)}), bf16[4,160,2048]{2,1,0:T(8,128)(2,1)S(1)}, u32[]{:S(2)}, u32[]{:S(2)}) async-start(bf16[4,160,2048]{2,1,0:T(8,128)(2,1)} %get-tuple-element.45), calls=%async_computation.1 | async-start | bytes 5242880 | tf_op jit(solution)/shard_map/all_to_all | solution.py:421
  102.9 19.0 %far.1 = (bf16[1536,512]{1,0:T(8,128)(2,1)}, bf16[1536,512]{1,0:T(8,128)(2,1)}, f32[256,512]{1,0:T(8,128)}, bf16[3,256,512]{2,1,0:T(8,128)(2,1)}, bf16[3,256,512]{2,1,0:T(8,128)(2,1)}) custom-call(s32[8]{0:T(128)} %multiply_subtract_fusion.gaps_ref, bf16[256,2048]{1,0:T(8,128)(2,1)} %q_ref.11, bf16[256,2048]{1,0:T(8,128)(2,1)} %do_ref.11, ...), custom_call_target="tpu_custom_call" | custom-call | flops 10871635968 | bytes 7864320 | tf_op jit(solution)/shard_map/far/pallas_call | solution.py:362
  121.9 2.0 %collective-permute-start.10 = (bf16[3,256,512]{2,1,0:T(8,128)(2,1)}, bf16[3,256,512]{2,1,0:T(8,128)(2,1)S(1)}, u32[]{:S(2)}, u32[]{:S(2)}) collective-permute-start(bf16[3,256,512]{2,1,0:T(8,128)(2,1)} %get-tuple-element.50), channel_id=1, source_target_pairs={{0,1},{1,0},{2,3},{3,2},{4,5},{5,4},{6,7},{7,6},{8,9},{9,8},{10,11... | collective-permute-start | bytes 2359304 | tf_op jit(solution)/shard_map/ppermute | solution.py:30
  123.9 1.6 convert_reduce_fusion.2
  127.1 3.5 %collective-permute-start.12 = (bf16[256,512]{1,0:T(8,128)(2,1)}, bf16[256,512]{1,0:T(8,128)(2,1)}, u32[]{:S(2)}, u32[]{:S(2)}) collective-permute-start(bf16[256,512]{1,0:T(8,128)(2,1)} %get-tuple-element.66), channel_id=1, source_target_pairs={{0,4},{1,5},{2,6},{3,7},{4,0},{5,1},{6,2},{7,3},{8,12},{9,13},{10,... | collective-permute-start | bytes 786440 | tf_op jit(solution)/shard_map/ppermute | solution.py:30
  130.7 14.1 %near.1 = (bf16[4,160,1024]{2,1,0:T(8,128)(2,1)}, bf16[1,256,512]{2,1,0:T(8,128)(2,1)}, bf16[1,256,512]{2,1,0:T(8,128)(2,1)}) custom-call(s32[8]{0:T(128)} %multiply_subtract_fusion.gaps_ref, bf16[256,2048]{1,0:T(8,128)(2,1)} %q_ref.11, bf16[256,2048]{1,0:T(8,128)(2,1)} %do_ref.11, f32[8,8,256]{2,1,0:T(8,128)} %get-tuple-element.36.refs_0_, ...), custom_call_target="tpu_custom_call" | custom-call | flops 3623878656 | bytes 2621440 | tf_op jit(solution)/shard_map/near/pallas_call | solution.py:362
  144.8 4.3 %all-to-all-start.2 = ((bf16[4,160,1024]{2,1,0:T(8,128)(2,1)}), bf16[4,160,1024]{2,1,0:T(8,128)(2,1)}, u32[]{:S(2)}, u32[]{:S(2)}) async-start(bf16[4,160,1024]{2,1,0:T(8,128)(2,1)} %get-tuple-element.56), calls=%async_computation.2 | async-start | bytes 2621440 | tf_op jit(solution)/shard_map/all_to_all | solution.py:430
  150.1 1.2 collective-permute-start.14
  151.4 1.1 collective-permute-done.14
  152.4 2.0 %fusion.1 = f32[256,512]{1,0:T(8,128)} fusion(bf16[256,512]{1,0:T(8,128)(2,1)} %collective-permute-done.13, bf16[256,512]{1,0:T(8,128)(2,1)} %collective-permute-done.12, bf16[256,512]{1,0:T(8,128)(2,1)S(1)} %collective-permute-done.11, bf16[1,256,512]{2,1,0:T(8,128)(2,1)S(1)} %collective-permute-done.14, bf16[1,256,512]{2,1,0:T(8,128)(2,1)S(1)} %copy-done.9), kind=kLoop, calls=%fused_computation.9 | loop fusion | flops 1179648 | bytes 1835008 | tf_op jit(solution)/shard_map/add | solution.py:435
  154.4 10.9 %all-to-all-done.2 = bf16[4,160,1024]{2,1,0:T(8,128)(2,1)} async-done(((bf16[4,160,1024]{2,1,0:T(8,128)(2,1)}), bf16[4,160,1024]{2,1,0:T(8,128)(2,1)}, u32[]{:S(2)}, u32[]{:S(2)}) %all-to-all-start.2) | async-done | bytes 1310752 | tf_op jit(solution)/shard_map/all_to_all | solution.py:430
  165.4 1.6 convert_reduce_fusion.1
  167.9 1.5 pad_maximum_fusion
  (62 shorter events, 10.1 us)
Async XLA Ops:
  0.6 4.0 %collective-permute-start.1 = (bf16[256,512]{1,0:T(8,128)(2,1)}, bf16[256,512]{1,0:T(8,128)(2,1)S(1)}, u32[]{:S(2)}, u32[]{:S(2)}) collective-permute-start(bf16[256,512]{1,0:T(8,128)(2,1)} %refs_6_.2), channel_id=1, source_target_pairs={{0,1},{1,0},{2,3},{3,2},{4,5},{5,4},{6,7},{7,6},{8,9},{9,8},{10,11... | collective-permute-start | bytes 786440 | tf_op jit(solution)/shard_map/ppermute | solution.py:30
  1.4 26.3 %collective-permute-start.3 = (bf16[256,512]{1,0:T(8,128)(2,1)}, bf16[256,512]{1,0:T(8,128)(2,1)S(1)}, u32[]{:S(2)}, u32[]{:S(2)}) collective-permute-start(bf16[256,512]{1,0:T(8,128)(2,1)} %refs_6_.2), channel_id=1, source_target_pairs={{0,4},{1,5},{2,6},{3,7},{4,0},{5,1},{6,2},{7,3},{8,12},{9,13},{10,... | collective-permute-start | bytes 786440 | tf_op jit(solution)/shard_map/ppermute | solution.py:30
  1.4 26.3 %collective-permute-start = (bf16[256,512]{1,0:T(8,128)(2,1)}, bf16[256,512]{1,0:T(8,128)(2,1)S(1)}, u32[]{:S(2)}, u32[]{:S(2)}) collective-permute-start(bf16[256,512]{1,0:T(8,128)(2,1)} %refs_6_.2), channel_id=1, source_target_pairs={{0,2},{1,3},{2,0},{3,1},{4,6},{5,7},{6,4},{7,5},{8,10},{9,11},{10,... | collective-permute-start | bytes 786440 | tf_op jit(solution)/shard_map/ppermute | solution.py:30
  2.7 24.9 %collective-permute-start.5 = (bf16[256,512]{1,0:T(8,128)(2,1)}, bf16[256,512]{1,0:T(8,128)(2,1)S(1)}, u32[]{:S(2)}, u32[]{:S(2)}) collective-permute-start(bf16[256,512]{1,0:T(8,128)(2,1)} %refs_6_.2), channel_id=1, source_target_pairs={{0,6},{1,7},{2,4},{3,5},{4,2},{5,3},{6,0},{7,1},{8,14},{9,15},{10,... | collective-permute-start | bytes 786440 | tf_op jit(solution)/shard_map/ppermute | solution.py:30
  27.6 2.5 %copy-start.8 = (bf16[256,512]{1,0:T(8,128)(2,1)}, bf16[256,512]{1,0:T(8,128)(2,1)S(1)}, u32[]{:S(2)}) copy-start(bf16[256,512]{1,0:T(8,128)(2,1)S(1)} %collective-permute-done.5.refs_4_) | copy-start | bytes 786436
  27.6 2.4 %copy-start.6 = (bf16[256,512]{1,0:T(8,128)(2,1)}, bf16[256,512]{1,0:T(8,128)(2,1)S(1)}, u32[]{:S(2)}) copy-start(bf16[256,512]{1,0:T(8,128)(2,1)S(1)} %collective-permute-done.3.refs_2_) | copy-start | bytes 786436
  27.6 2.4 %copy-start.7 = (bf16[256,512]{1,0:T(8,128)(2,1)}, bf16[256,512]{1,0:T(8,128)(2,1)S(1)}, u32[]{:S(2)}) copy-start(bf16[256,512]{1,0:T(8,128)(2,1)S(1)} %collective-permute-done.refs_0_) | copy-start | bytes 786436
  27.7 1.7 collective-permute-start.2
  28.2 1.5 collective-permute-start.4
  28.2 1.8 %collective-permute-start.6 = (bf16[256,512]{1,0:T(8,128)(2,1)S(1)}, bf16[256,512]{1,0:T(8,128)(2,1)S(1)}, u32[]{:S(2)}, u32[]{:S(2)}) collective-permute-start(bf16[256,512]{1,0:T(8,128)(2,1)S(1)} %collective-permute-done.5.refs_4_), channel_id=1, source_target_pairs={{0,1},{1,0},{2,3},{3,2},{4,5},{5,4},{6,7},{7,6},{8,9},{9,8},{10,11... | collective-permute-start | bytes 786440 | tf_op jit(solution)/shard_map/ppermute | solution.py:30
  50.9 6.2 %collective-permute-start.9 = (f32[8,8,256]{2,1,0:T(8,128)}, f32[8,8,256]{2,1,0:T(8,128)S(1)}, u32[]{:S(2)}, u32[]{:S(2)}) collective-permute-start(f32[8,8,256]{2,1,0:T(8,128)} %get-tuple-element.36.refs_0_), channel_id=1, source_target_pairs={{0,24},{8,16},{16,8},{24,0},{1,25},{9,17},{17,9},{25,1},{2,26},{10... | collective-permute-start | bytes 196616 | tf_op jit(solution)/shard_map/ppermute | solution.py:30
  53.1 4.0 %collective-permute-start.8 = (f32[8,8,256]{2,1,0:T(8,128)}, f32[8,8,256]{2,1,0:T(8,128)S(1)}, u32[]{:S(2)}, u32[]{:S(2)}) collective-permute-start(f32[8,8,256]{2,1,0:T(8,128)} %get-tuple-element.36.refs_0_), channel_id=1, source_target_pairs={{0,16},{8,24},{16,0},{24,8},{1,17},{9,25},{17,1},{25,9},{2,18},{10... | collective-permute-start | bytes 196616 | tf_op jit(solution)/shard_map/ppermute | solution.py:30
  53.4 3.8 %collective-permute-start.7 = (f32[8,8,256]{2,1,0:T(8,128)}, f32[8,8,256]{2,1,0:T(8,128)S(1)}, u32[]{:S(2)}, u32[]{:S(2)}) collective-permute-start(f32[8,8,256]{2,1,0:T(8,128)} %get-tuple-element.36.refs_0_), channel_id=1, source_target_pairs={{0,8},{8,0},{16,24},{24,16},{1,9},{9,1},{17,25},{25,17},{2,10},{10... | collective-permute-start | bytes 196616 | tf_op jit(solution)/shard_map/ppermute | solution.py:30
  71.4 26.7 %all-to-all-start = ((bf16[4,160,1024]{2,1,0:T(8,128)(2,1)}), bf16[4,160,1024]{2,1,0:T(8,128)(2,1)S(1)}, u32[]{:S(2)}, u32[]{:S(2)}) async-start(bf16[4,160,1024]{2,1,0:T(8,128)(2,1)} %get-tuple-element.42), calls=%async_computation | async-start | bytes 2621440 | tf_op jit(solution)/shard_map/all_to_all | solution.py:421
  98.1 1.1 copy-start
  99.2 45.6 %all-to-all-start.1 = ((bf16[4,160,2048]{2,1,0:T(8,128)(2,1)}), bf16[4,160,2048]{2,1,0:T(8,128)(2,1)S(1)}, u32[]{:S(2)}, u32[]{:S(2)}) async-start(bf16[4,160,2048]{2,1,0:T(8,128)(2,1)} %get-tuple-element.45), calls=%async_computation.1 | async-start | bytes 5242880 | tf_op jit(solution)/shard_map/all_to_all | solution.py:421
  121.9 4.1 %copy-start.1 = (bf16[3,256,512]{2,1,0:T(8,128)(2,1)S(1)}, bf16[3,256,512]{2,1,0:T(8,128)(2,1)}, u32[]{:S(2)}) copy-start(bf16[3,256,512]{2,1,0:T(8,128)(2,1)} %get-tuple-element.49) | copy-start | bytes 2359300
  121.9 4.1 %collective-permute-start.10 = (bf16[3,256,512]{2,1,0:T(8,128)(2,1)}, bf16[3,256,512]{2,1,0:T(8,128)(2,1)S(1)}, u32[]{:S(2)}, u32[]{:S(2)}) collective-permute-start(bf16[3,256,512]{2,1,0:T(8,128)(2,1)} %get-tuple-element.50), channel_id=1, source_target_pairs={{0,1},{1,0},{2,3},{3,2},{4,5},{5,4},{6,7},{7,6},{8,9},{9,8},{10,11... | collective-permute-start | bytes 2359304 | tf_op jit(solution)/shard_map/ppermute | solution.py:30
  127.1 22.5 %collective-permute-start.11 = (bf16[256,512]{1,0:T(8,128)(2,1)}, bf16[256,512]{1,0:T(8,128)(2,1)S(1)}, u32[]{:S(2)}, u32[]{:S(2)}) collective-permute-start(bf16[256,512]{1,0:T(8,128)(2,1)} %get-tuple-element.64), channel_id=1, source_target_pairs={{0,2},{1,3},{2,0},{3,1},{4,6},{5,7},{6,4},{7,5},{8,10},{9,11},{10,... | collective-permute-start | bytes 786440 | tf_op jit(solution)/shard_map/ppermute | solution.py:30
  127.1 22.5 %collective-permute-start.13 = (bf16[256,512]{1,0:T(8,128)(2,1)}, bf16[256,512]{1,0:T(8,128)(2,1)}, u32[]{:S(2)}, u32[]{:S(2)}) collective-permute-start(bf16[256,512]{1,0:T(8,128)(2,1)} %get-tuple-element.65), channel_id=1, source_target_pairs={{0,6},{1,7},{2,4},{3,5},{4,2},{5,3},{6,0},{7,1},{8,14},{9,15},{10,... | collective-permute-start | bytes 786440 | tf_op jit(solution)/shard_map/ppermute | solution.py:30
  127.1 22.8 %collective-permute-start.12 = (bf16[256,512]{1,0:T(8,128)(2,1)}, bf16[256,512]{1,0:T(8,128)(2,1)}, u32[]{:S(2)}, u32[]{:S(2)}) collective-permute-start(bf16[256,512]{1,0:T(8,128)(2,1)} %get-tuple-element.66), channel_id=1, source_target_pairs={{0,4},{1,5},{2,6},{3,7},{4,0},{5,1},{6,2},{7,3},{8,12},{9,13},{10,... | collective-permute-start | bytes 786440 | tf_op jit(solution)/shard_map/ppermute | solution.py:30
  144.8 20.6 %all-to-all-start.2 = ((bf16[4,160,1024]{2,1,0:T(8,128)(2,1)}), bf16[4,160,1024]{2,1,0:T(8,128)(2,1)}, u32[]{:S(2)}, u32[]{:S(2)}) async-start(bf16[4,160,1024]{2,1,0:T(8,128)(2,1)} %get-tuple-element.56), calls=%async_computation.2 | async-start | bytes 2621440 | tf_op jit(solution)/shard_map/all_to_all | solution.py:430
  149.6 2.8 %copy-start.9 = (bf16[1,256,512]{2,1,0:T(8,128)(2,1)S(1)}, bf16[1,256,512]{2,1,0:T(8,128)(2,1)}, u32[]{:S(2)}) copy-start(bf16[1,256,512]{2,1,0:T(8,128)(2,1)} %get-tuple-element.57) | copy-start | bytes 786436
  150.1 2.4 %collective-permute-start.14 = (bf16[1,256,512]{2,1,0:T(8,128)(2,1)S(1)}, bf16[1,256,512]{2,1,0:T(8,128)(2,1)S(1)}, u32[]{:S(2)}, u32[]{:S(2)}) collective-permute-start(bf16[1,256,512]{2,1,0:T(8,128)(2,1)S(1)} %copy-done.13), channel_id=1, source_target_pairs={{0,1},{1,0},{2,3},{3,2},{4,5},{5,4},{6,7},{7,6},{8,9},{9,8},{10,11... | collective-permute-start | bytes 786440 | tf_op jit(solution)/shard_map/ppermute | solution.py:30
  (8 other events, 5.7 us)

commit v3 on v2

--- a/solution.py
+++ b/solution.py
@@ -187,75 +187,42 @@
     up_grads(pl.program_id(0), terms, gq, out_ref)
 
 
-def add_latent(gl_ref, own, other):
-    total = gl_ref[...]
-    for gk, gv, uk, uv in [own, other] if own else [other]:
-        total = total + dot(gk[...], uk[...], NT) + dot(gv[...], uv[...], NT)
-    gl_ref[...] = total
-
-
-def put_latent(gl_ref, keep_ref, send_ref):
+def add_latent(gl_ref, own, other, keep_ref, send_ref):
+    step = pl.program_id(0)
     steps, rb, _ = keep_ref.shape
-    for i in range(steps):
-        keep_ref[i] = gl_ref[2 * i * rb : (2 * i + 1) * rb, :].astype(BF16)
-        send_ref[i] = gl_ref[(2 * i + 1) * rb : (2 * i + 2) * rb, :].astype(BF16)
-
-
-def far_kernel(n, chunks, own, gaps_ref, q_ref, do_ref, *refs):
+    for i in range(2 * steps):
+        rows = pl.ds(i * rb, rb)
+        total = jnp.where(step == 0, 0.0, gl_ref[rows, :])
+        for gk, gv, uk, uv in (own, other):
+            total = total + dot(gk[rows, :], uk[...], NT) + dot(gv[rows, :], uv[...], NT)
+        gl_ref[rows, :] = total
+        out_ref = send_ref if i % 2 else keep_ref
+        out_ref[i // 2] = total.astype(BF16)
+
+
+def far_kernel(n, chunks, gaps_ref, q_ref, do_ref, *refs):
     st_refs, refs = refs[:n], refs[n:]
     k_refs, v_refs, refs = refs[: len(chunks)], refs[len(chunks) : 2 * len(chunks)], refs[2 * len(chunks) :]
     uk_ref, uv_ref, uk2_ref, uv2_ref, ok_ref, ov_ref, gk_ref, gv_ref, gq_ref, keep_ref, send_ref, gl_ref = refs
-    step = pl.program_id(0)
-
-    @pl.when(step == 0)
-    def _():
-        gl_ref[...] = jnp.zeros_like(gl_ref)
-
-    @pl.when(step < own)
-    def _():
-        blocks = [(c, k, v, 0, k.shape[1]) for c, k, v in zip(chunks, k_refs, v_refs)]
-        gq_ref[...] = head_grads(gaps_ref, q_ref, do_ref, st_refs, blocks, gk_ref, gv_ref)
-        add_latent(gl_ref, (gk_ref, gv_ref, uk_ref, uv_ref), (ok_ref, ov_ref, uk2_ref, uv2_ref))
-
-    @pl.when(step >= own)
-    def _():
-        add_latent(gl_ref, None, (ok_ref, ov_ref, uk2_ref, uv2_ref))
-
-    @pl.when(step == pl.num_programs(0) - 1)
-    def _():
-        put_latent(gl_ref, keep_ref, send_ref)
-
-
-def near_kernel(n, chunks, own, gaps_ref, q_ref, do_ref, *refs):
+    blocks = [(c, k, v, 0, k.shape[1]) for c, k, v in zip(chunks, k_refs, v_refs)]
+    gq_ref[...] = head_grads(gaps_ref, q_ref, do_ref, st_refs, blocks, gk_ref, gv_ref)
+    add_latent(gl_ref, (gk_ref, gv_ref, uk_ref, uv_ref), (ok_ref, ov_ref, uk2_ref, uv2_ref), keep_ref, send_ref)
+
+
+def near_kernel(n, chunks, gaps_ref, q_ref, do_ref, *refs):
     st_refs, refs = refs[:n], refs[n:]
     k_refs, v_refs, refs = refs[: len(chunks)], refs[len(chunks) : 2 * len(chunks)], refs[2 * len(chunks) :]
     uk_ref, uv_ref, uk2_ref, uv2_ref, ok_ref, ov_ref, latt_ref, fk_ref, fv_ref, fq_ref = refs[:10]
     out_ref, keep_ref, send_ref, gk_ref, gv_ref, gl_ref = refs[10:]
-    step = pl.program_id(0)
-
-    @pl.when(step == 0)
-    def _():
-        gl_ref[...] = jnp.zeros_like(gl_ref)
-
-    @pl.when(step < own)
-    def _():
-        blocks = [(c, k, v, 0, k.shape[1]) for c, k, v in zip(chunks, k_refs, v_refs)]
-        gq = fq_ref[...] + head_grads(gaps_ref, q_ref, do_ref, st_refs, blocks, gk_ref, gv_ref)
-        rest = fk_ref.shape[0]
-        terms = [
-            (latt_ref[:, :rest], (fk_ref[...], fv_ref[...])),
-            (latt_ref[:, rest:], (gk_ref[...], gv_ref[...])),
-        ]
-        up_grads(step, terms, gq, out_ref)
-        add_latent(gl_ref, (gk_ref, gv_ref, uk_ref, uv_ref), (ok_ref, ov_ref, uk2_ref, uv2_ref))
-
-    @pl.when(step >= own)
-    def _():
-        add_latent(gl_ref, None, (ok_ref, ov_ref, uk2_ref, uv2_ref))
-
-    @pl.when(step == pl.num_programs(0) - 1)
-    def _():
-        put_latent(gl_ref, keep_ref, send_ref)
+    blocks = [(c, k, v, 0, k.shape[1]) for c, k, v in zip(chunks, k_refs, v_refs)]
+    gq = fq_ref[...] + head_grads(gaps_ref, q_ref, do_ref, st_refs, blocks, gk_ref, gv_ref)
+    rest = fk_ref.shape[0]
+    terms = [
+        (latt_ref[:, :rest], (fk_ref[...], fv_ref[...])),
+        (latt_ref[:, rest:], (gk_ref[...], gv_ref[...])),
+    ]
+    up_grads(pl.program_id(0), terms, gq, out_ref)
+    add_latent(gl_ref, (gk_ref, gv_ref, uk_ref, uv_ref), (ok_ref, ov_ref, uk2_ref, uv2_ref), keep_ref, send_ref)
 
 
 def turn_kernel(*refs):
@@ -322,25 +289,24 @@
     qn = queries.shape[0]
     wide = PAIR * HD
     cols = pairs * wide
-    last = pairs - 1
-    own = lambda g, *_: (0, first + jnp.minimum(g, last))
-    own3 = lambda g, *_: (first + jnp.minimum(g, last), 0, 0)
-    out = lambda g, *_: (0, jnp.minimum(g, last))
-    col = lambda g, *_: (0, g)
+    span = first // pairs * wide
+    own = lambda g, *_: (0, first + g)
+    own3 = lambda g, *_: (first + g, 0, 0)
+    out = col = lambda g, *_: (0, g)
     fixed = lambda g, *_: (0, 0)
     fixed3 = lambda g, *_: (0, 0, 0)
 
     def rows_of(chunk):
         if chunk == 0:
             return 0, own3
-        return 1, lambda g, *_: (first + jnp.minimum(g, last), chunk - 1, 0)
+        return 1, lambda g, *_: (first + g, chunk - 1, 0)
 
     picked = [rows_of(c) for c in chunks]
     in_specs = [pl.BlockSpec((qn, wide), own)] * 2 + [pl.BlockSpec((None, 8, qn), own3)] * n
     in_specs += [pl.BlockSpec((PAIR, size, 2 * HD), index) for _, index in picked]
     in_specs += [pl.BlockSpec((PAIR, size, HD), index) for _, index in picked]
-    in_specs += [pl.BlockSpec((depth, wide), own)] * 2 + [pl.BlockSpec((depth, wide), col)] * 2
-    in_specs += [pl.BlockSpec((rows, wide), lambda g, *_: (0 if far else other[0].shape[0] // rows - 1, g))] * 2
+    in_specs += [pl.BlockSpec((depth, wide), own)] * 2 + [pl.BlockSpec((depth, span), col)] * 2
+    in_specs += [pl.BlockSpec((rows, span), lambda g, *_: (0 if far else other[0].shape[0] // rows - 1, g))] * 2
     grads = (jax.ShapeDtypeStruct((rows, cols), BF16),) * 2
     sums = (jax.ShapeDtypeStruct((len(chunks), rb, depth), BF16),) * 2
     sum_specs = [pl.BlockSpec(sums[0].shape, fixed3)] * 2
@@ -360,11 +326,11 @@
         scratch = [pltpu.VMEM((rows, wide), BF16)] * 2
         scratch += [gl]
     return pl.pallas_call(
-        functools.partial(kernel, n, chunks, pairs),
+        functools.partial(kernel, n, chunks),
         out_shape=out_shape,
         grid_spec=pltpu.PrefetchScalarGridSpec(
             num_scalar_prefetch=1,
-            grid=(first,),
+            grid=(pairs,),
             in_specs=in_specs,
             out_specs=out_specs,
             scratch_shapes=scratch,
@@ -413,28 +379,27 @@
 
     pairs = heads // PAIR
     first = 3 * pairs // 4
-    half = first // 3
     held, outs = (), []
-    for lower, upper in ((0, half), (half, first)):
+    for lower, upper in ((0, first),):
         gk, gv, part = run_whole(gaps, queries, grad_out, stats, k2, v, latt, lower, upper, first, held)
         held = (gk, gv)
         outs.append(lax.all_to_all(part, "ctx", 0, 0, tiled=True))
     split = functools.partial(run_split, up_key=up_key, up_value=up_value, other=(gk, gv), first=first,
                               pairs=pairs - first, queries=queries, grad_out=grad_out, stats=stats, k2=k2, v=v)
-    fk, fv, fq, far, far_away = split(True, after(gaps, outs[0]), chunks=list(range(near, chunks)))
+    fk, fv, fq, far, far_away = split(True, gaps, chunks=list(range(near, chunks)))
     far = far.astype(F32) + swap(far_away, "head", 1).astype(F32)
     far = far.astype(BF16)
     part, close, close_away = split(
         False, after(gaps, far), chunks=list(range(near)), latt=latt, before=(fk, fv, fq)
     )
-    outs.append(lax.all_to_all(after(part, outs[1]), "ctx", 0, 0, tiled=True))
+    outs.append(lax.all_to_all(after(part, outs[0]), "ctx", 0, 0, tiled=True))
     got = [swap(far[k], "head", 2 * (near + k)) for k in range(chunks - near)]
-    close = close.astype(F32) + swap(after(close_away, *got), "head", 1).astype(F32)
+    close = close.astype(F32) + swap(after(close_away, outs[1], *got), "head", 1).astype(F32)
     grad_latent = close[0]
     for x in got:
         grad_latent = grad_latent + x.astype(F32)
 
-    sums = [jnp.sum(o.astype(F32), axis=0) for o in outs]
+    sums = [functools.reduce(jnp.add, [o[k].astype(F32) for k in range(n)]) for o in outs]
     ub = depth // n
     grad_key = jnp.concatenate([s[:ub, : s.shape[1] // 2] for s in sums], axis=1)
     grad_value = jnp.concatenate([s[:ub, s.shape[1] // 2 :] for s in sums], axis=1)

time: 172 us -> 165 us (0.959); the launches traced: 169 us -> 165 us
  Pallas kernels: 103 us -> 94 us
  waiting for transfers between devices: 26.7 us -> 34.6 us
  starting transfers between devices: 25.6 us -> 22.4 us
    all_to_all x2 -> x1, waiting for transfers between devices: 0.01 us -> 5.38 us  [local(): outs.append(lax.all_to_all(part, 'ctx', 0, 0, tiled=True))]
    pallas_call x2 -> x1, Pallas kernels: 36.6 us -> 31.6 us  [run_whole(): pl.pallas_call(functools.partial(whole_kernel, n, len(held)), out_shape=(...]
    reduce_sum x3 -> x0, other arithmetic: 3.76 us -> none  [local(): sums = [jnp.sum(o.astype(F32), axis=0) for o in outs]]
    pallas_call x2, Pallas kernels: 33.1 us -> 29.4 us  [run_split(): pl.pallas_call(functools.partial(kernel, n, chunks), out_shape=out_shape,...]
    add x0 -> x2, other arithmetic: none -> 2.9 us  [local(): functools.reduce(jnp.add, [o[k].astype(F32) for k in range(n)])]
    all_to_all x2 -> x1, starting transfers between devices: 7.38 us -> 4.98 us  [local(): outs.append(lax.all_to_all(part, 'ctx', 0, 0, tiled=True))]
    all_to_all x1, waiting for transfers between devices: 10.9 us -> 13 us  [local(): outs.append(lax.all_to_all(after(part, outs[0]), 'ctx', 0, 0, tiled=True))]
    unnamed x28 -> x24, local copies, waits for them, and re-layouts: 3.61 us -> 3.02 us
  transfers between devices with their start and end apart: 18 -> 17, of which waited for: 8 -> 7; matrix products, arithmetic and copies ran while one was open for 4% -> 5% of each run, Pallas kernels for 41% -> 26%
where the time goes in v3:
time: 165 us
  Pallas kernels  94 us (57%)
  waiting for transfers between devices  34.6 us (21%)
  starting transfers between devices  22.4 us (14%)
  other arithmetic  9.05 us (5%)
  local copies, waits for them, and re-layouts  4.09 us (2%)
    pallas_call x1, Pallas kernels, run_whole(): pl.pallas_call(functools.partial(whole_kernel, n, len(held)), out_shape=(...  31.6 us
    pallas_call x2, Pallas kernels, run_stats(): pl.pallas_call(functools.partial(stats_kernel, first, len(pieces)), out_s...  29.5 us
    pallas_call x2, Pallas kernels, run_split(): pl.pallas_call(functools.partial(kernel, n, chunks), out_shape=out_shape,...  29.4 us
    ppermute x15, waiting for transfers between devices, swap(): return lax.ppermute(array, axis, [(i, i ^ distance) for i in range(count)])  16.3 us
    ppermute x15, starting transfers between devices, swap(): return lax.ppermute(array, axis, [(i, i ^ distance) for i in range(count)])  13.9 us
    all_to_all x1, waiting for transfers between devices, local(): outs.append(lax.all_to_all(after(part, outs[0]), 'ctx', 0, 0, tiled=True))  13 us
    all_to_all x1, waiting for transfers between devices, local(): outs.append(lax.all_to_all(part, 'ctx', 0, 0, tiled=True))  5.38 us
    all_to_all x1, starting transfers between devices, local(): outs.append(lax.all_to_all(part, 'ctx', 0, 0, tiled=True))  4.98 us
  transfers between devices with their start and end apart: 17, of which 7 were waited for; matrix products, arithmetic and copies ran while one was open for 5% of the time, Pallas kernels for 26%

profile of v3, /device:TPU:17, one launch (start us, length us, event | category | flops | bytes accessed | tf_op | source)
XLA Modules:
  0.0 164.9 jit_solution(5304485994031402060)
XLA Ops:
  1.4 1.4 collective-permute-start
  2.7 1.3 collective-permute-start.5
  5.2 9.7 %stats.2 = (bf16[16,512,256]{2,1,0:T(8,128)(2,1)}, bf16[16,512,128]{2,1,0:T(8,128)(2,1)}, f32[8,8,256]{2,1,0:T(8,128)}) custom-call(s32[8]{0:T(128)} %multiply_subtract_fusion.gaps_ref, bf16[512,2048]{1,0:T(8,128)(2,1)} %refs_8_.1, bf16[512,2048]{1,0:T(8,128)(2,1)} %refs_9_.1, bf16[256,2048]{1,0:T(8,128)(2,1)} %q_ref.9, bf16[256,2048]{1,0:T(8,128)(2,1)} %do_ref.9, ...), custom_call_target="tpu_custom_call" | custom-call | flops 4294967296 | bytes 6291456 | tf_op jit(solution)/shard_map/stats/pallas_call | solution.py:98
  14.9 12.7 %collective-permute-done.5.refs_4_ = bf16[256,512]{1,0:T(8,128)(2,1)S(1)} collective-permute-done((bf16[256,512]{1,0:T(8,128)(2,1)}, bf16[256,512]{1,0:T(8,128)(2,1)S(1)}, u32[]{:S(2)}, u32[]{:S(2)}) %collective-permute-start.5) | collective-permute-done | bytes 262176 | tf_op jit(solution)/shard_map/ppermute | solution.py:30
  31.1 19.8 %stats.3 = (bf16[16,1536,256]{2,1,0:T(8,128)(2,1)}, bf16[16,1536,128]{2,1,0:T(8,128)(2,1)}, f32[8,8,256]{2,1,0:T(8,128)}) custom-call(s32[8]{0:T(128)} %multiply_subtract_fusion.gaps_ref, bf16[512,2048]{1,0:T(8,128)(2,1)} %refs_8_.1, bf16[512,2048]{1,0:T(8,128)(2,1)} %refs_9_.1, bf16[256,2048]{1,0:T(8,128)(2,1)} %q_ref.9, bf16[256,2048]{1,0:T(8,128)(2,1)} %do_ref.9, ...), custom_call_target="tpu_custom_call" | custom-call | flops 12884901888 | bytes 18874368 | tf_op jit(solution)/shard_map/stats/pallas_call | solution.py:98
  50.9 2.2 %collective-permute-start.9 = (f32[8,8,256]{2,1,0:T(8,128)}, f32[8,8,256]{2,1,0:T(8,128)S(1)}, u32[]{:S(2)}, u32[]{:S(2)}) collective-permute-start(f32[8,8,256]{2,1,0:T(8,128)} %get-tuple-element.32.refs_0_), channel_id=1, source_target_pairs={{0,24},{8,16},{16,8},{24,0},{1,25},{9,17},{17,9},{25,1},{2,26},{10... | collective-permute-start | bytes 196616 | tf_op jit(solution)/shard_map/ppermute | solution.py:30
  53.6 3.5 %turn.1.refs_8_.refs_12_ = bf16[512,2048]{1,0:T(8,128)(2,1)} custom-call(bf16[256,512]{1,0:T(8,128)(2,1)} %copy-done.3, bf16[256,512]{1,0:T(8,128)(2,1)} %copy-done.5, bf16[256,512]{1,0:T(8,128)(2,1)} %copy-done.2, bf16[256,512]{1,0:T(8,128)(2,1)} %copy-done.6, bf16[256,512]{1,0:T(8,128)(2,1)} %copy-done.4, bf16[256,512]{1,0:T(8,128)(2,1)} %copy-done.7, ...), custom_call_target="tpu_custom_call" | custom-call | tf_op jit(solution)/shard_map/turn/pallas_call | solution.py:236
  57.8 31.6 %whole.1 = (bf16[2048,1536]{1,0:T(8,128)(2,1)}, bf16[2048,1536]{1,0:T(8,128)(2,1)}, bf16[4,160,3072]{2,1,0:T(8,128)(2,1)}) custom-call(s32[8]{0:T(128)} %multiply_subtract_fusion.gaps_ref, bf16[256,2048]{1,0:T(8,128)(2,1)} %q_ref.9, bf16[256,2048]{1,0:T(8,128)(2,1)} %do_ref.9, f32[8,8,256]{2,1,0:T(8,128)} %get-tuple-element.32.refs_0_, ...), custom_call_target="tpu_custom_call" | custom-call | flops 17716740096 | bytes 31457280 | tf_op jit(solution)/shard_map/whole/pallas_call | solution.py:259
  89.4 5.0 %all-to-all-start = ((bf16[4,160,3072]{2,1,0:T(8,128)(2,1)}), bf16[4,160,3072]{2,1,0:T(8,128)(2,1)}, u32[]{:S(2)}, u32[]{:S(2)}) async-start(bf16[4,160,3072]{2,1,0:T(8,128)(2,1)} %get-tuple-element.38), calls=%async_computation | async-start | bytes 7864320 | tf_op jit(solution)/shard_map/all_to_all | solution.py:386
  94.4 17.6 %far.1 = (bf16[1536,512]{1,0:T(8,128)(2,1)}, bf16[1536,512]{1,0:T(8,128)(2,1)}, f32[256,512]{1,0:T(8,128)}, bf16[3,256,512]{2,1,0:T(8,128)(2,1)}, bf16[3,256,512]{2,1,0:T(8,128)(2,1)}) custom-call(s32[8]{0:T(128)} %multiply_subtract_fusion.gaps_ref, bf16[256,2048]{1,0:T(8,128)(2,1)} %q_ref.9, bf16[256,2048]{1,0:T(8,128)(2,1)} %do_ref.9, ...), custom_call_target="tpu_custom_call" | custom-call | flops 10871635968 | bytes 7864320 | tf_op jit(solution)/shard_map/far/pallas_call | solution.py:328
  112.0 1.7 %collective-permute-start.10 = (bf16[3,256,512]{2,1,0:T(8,128)(2,1)}, bf16[3,256,512]{2,1,0:T(8,128)(2,1)S(1)}, u32[]{:S(2)}, u32[]{:S(2)}) collective-permute-start(bf16[3,256,512]{2,1,0:T(8,128)(2,1)} %get-tuple-element.42), channel_id=1, source_target_pairs={{0,1},{1,0},{2,3},{3,2},{4,5},{5,4},{6,7},{7,6},{8,9},{9,8},{10,11... | collective-permute-start | bytes 2359304 | tf_op jit(solution)/shard_map/ppermute | solution.py:30
  113.6 2.1 %collective-permute-done.10 = bf16[3,256,512]{2,1,0:T(8,128)(2,1)S(1)} collective-permute-done((bf16[3,256,512]{2,1,0:T(8,128)(2,1)}, bf16[3,256,512]{2,1,0:T(8,128)(2,1)S(1)}, u32[]{:S(2)}, u32[]{:S(2)}) %collective-permute-start.10) | collective-permute-done | bytes 786464 | tf_op jit(solution)/shard_map/ppermute | solution.py:30
  115.7 1.3 add_convert_fusion
  117.1 0.9 slice_bitcast_fusion.2
  118.0 3.5 %collective-permute-start.12 = (bf16[256,512]{1,0:T(8,128)(2,1)}, bf16[256,512]{1,0:T(8,128)(2,1)}, u32[]{:S(2)}, u32[]{:S(2)}) collective-permute-start(bf16[256,512]{1,0:T(8,128)(2,1)} %get-tuple-element.58), channel_id=1, source_target_pairs={{0,4},{1,5},{2,6},{3,7},{4,0},{5,1},{6,2},{7,3},{8,12},{9,13},{10,... | collective-permute-start | bytes 786440 | tf_op jit(solution)/shard_map/ppermute | solution.py:30
  121.5 11.9 %near.1 = (bf16[4,160,1024]{2,1,0:T(8,128)(2,1)}, bf16[1,256,512]{2,1,0:T(8,128)(2,1)}, bf16[1,256,512]{2,1,0:T(8,128)(2,1)}) custom-call(s32[8]{0:T(128)} %multiply_subtract_fusion.gaps_ref, bf16[256,2048]{1,0:T(8,128)(2,1)} %q_ref.9, bf16[256,2048]{1,0:T(8,128)(2,1)} %do_ref.9, f32[8,8,256]{2,1,0:T(8,128)} %get-tuple-element.32.refs_0_, ...), custom_call_target="tpu_custom_call" | custom-call | flops 3623878656 | bytes 2621440 | tf_op jit(solution)/shard_map/near/pallas_call | solution.py:328
  133.4 5.4 %all-to-all-done = bf16[4,160,3072]{2,1,0:T(8,128)(2,1)} async-done(((bf16[4,160,3072]{2,1,0:T(8,128)(2,1)}), bf16[4,160,3072]{2,1,0:T(8,128)(2,1)}, u32[]{:S(2)}, u32[]{:S(2)}) %all-to-all-start) | async-done | bytes 3932192 | tf_op jit(solution)/shard_map/all_to_all | solution.py:386
  138.8 3.5 %all-to-all-start.1 = ((bf16[4,160,1024]{2,1,0:T(8,128)(2,1)}), bf16[4,160,1024]{2,1,0:T(8,128)(2,1)S(1)}, u32[]{:S(2)}, u32[]{:S(2)}) async-start(bf16[4,160,1024]{2,1,0:T(8,128)(2,1)} %get-tuple-element.48), calls=%async_computation.1 | async-start | bytes 2621440 | tf_op jit(solution)/shard_map/all_to_all | solution.py:395
  142.3 2.7 %add_bitcast_fusion = f32[160,3072]{1,0:T(8,128)S(1)} fusion(bf16[4,160,3072]{2,1,0:T(8,128)(2,1)} %all-to-all-done), kind=kLoop, calls=%fused_computation | loop fusion | flops 3440640 | bytes 5898240 | tf_op jit(solution)/shard_map/add | solution.py:402
  145.2 13.0 %all-to-all-done.1 = bf16[4,160,1024]{2,1,0:T(8,128)(2,1)S(1)} async-done(((bf16[4,160,1024]{2,1,0:T(8,128)(2,1)}), bf16[4,160,1024]{2,1,0:T(8,128)(2,1)S(1)}, u32[]{:S(2)}, u32[]{:S(2)}) %all-to-all-start.1) | async-done | bytes 1310752 | tf_op jit(solution)/shard_map/all_to_all | solution.py:395
  159.1 1.5 collective-permute-start.14
  160.6 0.8 maximum_maximum_fusion
  161.5 1.5 pad_maximum_fusion
  162.9 2.0 %fusion.1 = f32[256,512]{1,0:T(8,128)} fusion(bf16[256,512]{1,0:T(8,128)(2,1)} %collective-permute-done.13, bf16[256,512]{1,0:T(8,128)(2,1)} %collective-permute-done.12, bf16[256,512]{1,0:T(8,128)(2,1)S(1)} %collective-permute-done.11, bf16[1,256,512]{2,1,0:T(8,128)(2,1)S(1)} %collective-permute-done.14, bf16[1,256,512]{2,1,0:T(8,128)(2,1)S(1)} %copy-done), kind=kLoop, calls=%fused_computation.8 | loop fusion | flops 1179648 | bytes 1835008 | tf_op jit(solution)/shard_map/add | solution.py:400
  (52 shorter events, 7.6 us)
Async XLA Ops:
  0.6 3.9 %collective-permute-start.1 = (bf16[256,512]{1,0:T(8,128)(2,1)}, bf16[256,512]{1,0:T(8,128)(2,1)S(1)}, u32[]{:S(2)}, u32[]{:S(2)}) collective-permute-start(bf16[256,512]{1,0:T(8,128)(2,1)} %refs_6_.2), channel_id=1, source_target_pairs={{0,1},{1,0},{2,3},{3,2},{4,5},{5,4},{6,7},{7,6},{8,9},{9,8},{10,11... | collective-permute-start | bytes 786440 | tf_op jit(solution)/shard_map/ppermute | solution.py:30
  1.4 26.3 %collective-permute-start.3 = (bf16[256,512]{1,0:T(8,128)(2,1)}, bf16[256,512]{1,0:T(8,128)(2,1)S(1)}, u32[]{:S(2)}, u32[]{:S(2)}) collective-permute-start(bf16[256,512]{1,0:T(8,128)(2,1)} %refs_6_.2), channel_id=1, source_target_pairs={{0,4},{1,5},{2,6},{3,7},{4,0},{5,1},{6,2},{7,3},{8,12},{9,13},{10,... | collective-permute-start | bytes 786440 | tf_op jit(solution)/shard_map/ppermute | solution.py:30
  1.4 26.3 %collective-permute-start = (bf16[256,512]{1,0:T(8,128)(2,1)}, bf16[256,512]{1,0:T(8,128)(2,1)S(1)}, u32[]{:S(2)}, u32[]{:S(2)}) collective-permute-start(bf16[256,512]{1,0:T(8,128)(2,1)} %refs_6_.2), channel_id=1, source_target_pairs={{0,2},{1,3},{2,0},{3,1},{4,6},{5,7},{6,4},{7,5},{8,10},{9,11},{10,... | collective-permute-start | bytes 786440 | tf_op jit(solution)/shard_map/ppermute | solution.py:30
  2.7 24.9 %collective-permute-start.5 = (bf16[256,512]{1,0:T(8,128)(2,1)}, bf16[256,512]{1,0:T(8,128)(2,1)S(1)}, u32[]{:S(2)}, u32[]{:S(2)}) collective-permute-start(bf16[256,512]{1,0:T(8,128)(2,1)} %refs_6_.2), channel_id=1, source_target_pairs={{0,6},{1,7},{2,4},{3,5},{4,2},{5,3},{6,0},{7,1},{8,14},{9,15},{10,... | collective-permute-start | bytes 786440 | tf_op jit(solution)/shard_map/ppermute | solution.py:30
  27.6 2.5 %copy-start.4 = (bf16[256,512]{1,0:T(8,128)(2,1)}, bf16[256,512]{1,0:T(8,128)(2,1)S(1)}, u32[]{:S(2)}) copy-start(bf16[256,512]{1,0:T(8,128)(2,1)S(1)} %collective-permute-done.5.refs_4_) | copy-start | bytes 786436
  27.6 2.4 %copy-start.2 = (bf16[256,512]{1,0:T(8,128)(2,1)}, bf16[256,512]{1,0:T(8,128)(2,1)S(1)}, u32[]{:S(2)}) copy-start(bf16[256,512]{1,0:T(8,128)(2,1)S(1)} %collective-permute-done.3.refs_2_) | copy-start | bytes 786436
  27.6 2.4 %copy-start.3 = (bf16[256,512]{1,0:T(8,128)(2,1)}, bf16[256,512]{1,0:T(8,128)(2,1)S(1)}, u32[]{:S(2)}) copy-start(bf16[256,512]{1,0:T(8,128)(2,1)S(1)} %collective-permute-done.refs_0_) | copy-start | bytes 786436
  27.7 1.7 %collective-permute-start.2 = (bf16[256,512]{1,0:T(8,128)(2,1)S(1)}, bf16[256,512]{1,0:T(8,128)(2,1)S(1)}, u32[]{:S(2)}, u32[]{:S(2)}) collective-permute-start(bf16[256,512]{1,0:T(8,128)(2,1)S(1)} %collective-permute-done.refs_0_), channel_id=1, source_target_pairs={{0,1},{1,0},{2,3},{3,2},{4,5},{5,4},{6,7},{7,6},{8,9},{9,8},{10,11... | collective-permute-start | bytes 786440 | tf_op jit(solution)/shard_map/ppermute | solution.py:30
  28.2 1.5 collective-permute-start.4
  28.2 1.8 %collective-permute-start.6 = (bf16[256,512]{1,0:T(8,128)(2,1)S(1)}, bf16[256,512]{1,0:T(8,128)(2,1)S(1)}, u32[]{:S(2)}, u32[]{:S(2)}) collective-permute-start(bf16[256,512]{1,0:T(8,128)(2,1)S(1)} %collective-permute-done.5.refs_4_), channel_id=1, source_target_pairs={{0,1},{1,0},{2,3},{3,2},{4,5},{5,4},{6,7},{7,6},{8,9},{9,8},{10,11... | collective-permute-start | bytes 786440 | tf_op jit(solution)/shard_map/ppermute | solution.py:30
  29.3 0.8 copy-start.5
  30.4 0.7 copy-start.7
  50.9 6.2 %collective-permute-start.9 = (f32[8,8,256]{2,1,0:T(8,128)}, f32[8,8,256]{2,1,0:T(8,128)S(1)}, u32[]{:S(2)}, u32[]{:S(2)}) collective-permute-start(f32[8,8,256]{2,1,0:T(8,128)} %get-tuple-element.32.refs_0_), channel_id=1, source_target_pairs={{0,24},{8,16},{16,8},{24,0},{1,25},{9,17},{17,9},{25,1},{2,26},{10... | collective-permute-start | bytes 196616 | tf_op jit(solution)/shard_map/ppermute | solution.py:30
  53.1 4.0 %collective-permute-start.8 = (f32[8,8,256]{2,1,0:T(8,128)}, f32[8,8,256]{2,1,0:T(8,128)S(1)}, u32[]{:S(2)}, u32[]{:S(2)}) collective-permute-start(f32[8,8,256]{2,1,0:T(8,128)} %get-tuple-element.32.refs_0_), channel_id=1, source_target_pairs={{0,16},{8,24},{16,0},{24,8},{1,17},{9,25},{17,1},{25,9},{2,18},{10... | collective-permute-start | bytes 196616 | tf_op jit(solution)/shard_map/ppermute | solution.py:30
  53.4 3.8 %collective-permute-start.7 = (f32[8,8,256]{2,1,0:T(8,128)}, f32[8,8,256]{2,1,0:T(8,128)S(1)}, u32[]{:S(2)}, u32[]{:S(2)}) collective-permute-start(f32[8,8,256]{2,1,0:T(8,128)} %get-tuple-element.32.refs_0_), channel_id=1, source_target_pairs={{0,8},{8,0},{16,24},{24,16},{1,9},{9,1},{17,25},{25,17},{2,10},{10... | collective-permute-start | bytes 196616 | tf_op jit(solution)/shard_map/ppermute | solution.py:30
  89.4 49.4 %all-to-all-start = ((bf16[4,160,3072]{2,1,0:T(8,128)(2,1)}), bf16[4,160,3072]{2,1,0:T(8,128)(2,1)}, u32[]{:S(2)}, u32[]{:S(2)}) async-start(bf16[4,160,3072]{2,1,0:T(8,128)(2,1)} %get-tuple-element.38), calls=%async_computation | async-start | bytes 7864320 | tf_op jit(solution)/shard_map/all_to_all | solution.py:386
  112.0 3.8 %collective-permute-start.10 = (bf16[3,256,512]{2,1,0:T(8,128)(2,1)}, bf16[3,256,512]{2,1,0:T(8,128)(2,1)S(1)}, u32[]{:S(2)}, u32[]{:S(2)}) collective-permute-start(bf16[3,256,512]{2,1,0:T(8,128)(2,1)} %get-tuple-element.42), channel_id=1, source_target_pairs={{0,1},{1,0},{2,3},{3,2},{4,5},{5,4},{6,7},{7,6},{8,9},{9,8},{10,11... | collective-permute-start | bytes 2359304 | tf_op jit(solution)/shard_map/ppermute | solution.py:30
  118.0 40.5 %collective-permute-start.11 = (bf16[256,512]{1,0:T(8,128)(2,1)}, bf16[256,512]{1,0:T(8,128)(2,1)S(1)}, u32[]{:S(2)}, u32[]{:S(2)}) collective-permute-start(bf16[256,512]{1,0:T(8,128)(2,1)} %get-tuple-element.56), channel_id=1, source_target_pairs={{0,2},{1,3},{2,0},{3,1},{4,6},{5,7},{6,4},{7,5},{8,10},{9,11},{10,... | collective-permute-start | bytes 786440 | tf_op jit(solution)/shard_map/ppermute | solution.py:30
  118.0 40.5 %collective-permute-start.13 = (bf16[256,512]{1,0:T(8,128)(2,1)}, bf16[256,512]{1,0:T(8,128)(2,1)}, u32[]{:S(2)}, u32[]{:S(2)}) collective-permute-start(bf16[256,512]{1,0:T(8,128)(2,1)} %get-tuple-element.57), channel_id=1, source_target_pairs={{0,6},{1,7},{2,4},{3,5},{4,2},{5,3},{6,0},{7,1},{8,14},{9,15},{10,... | collective-permute-start | bytes 786440 | tf_op jit(solution)/shard_map/ppermute | solution.py:30
  118.0 40.5 %collective-permute-start.12 = (bf16[256,512]{1,0:T(8,128)(2,1)}, bf16[256,512]{1,0:T(8,128)(2,1)}, u32[]{:S(2)}, u32[]{:S(2)}) collective-permute-start(bf16[256,512]{1,0:T(8,128)(2,1)} %get-tuple-element.58), channel_id=1, source_target_pairs={{0,4},{1,5},{2,6},{3,7},{4,0},{5,1},{6,2},{7,3},{8,12},{9,13},{10,... | collective-permute-start | bytes 786440 | tf_op jit(solution)/shard_map/ppermute | solution.py:30
  138.8 19.4 %all-to-all-start.1 = ((bf16[4,160,1024]{2,1,0:T(8,128)(2,1)}), bf16[4,160,1024]{2,1,0:T(8,128)(2,1)S(1)}, u32[]{:S(2)}, u32[]{:S(2)}) async-start(bf16[4,160,1024]{2,1,0:T(8,128)(2,1)} %get-tuple-element.48), calls=%async_computation.1 | async-start | bytes 2621440 | tf_op jit(solution)/shard_map/all_to_all | solution.py:395
  158.2 1.0 copy-start.11
  159.1 3.8 %collective-permute-start.14 = (bf16[1,256,512]{2,1,0:T(8,128)(2,1)S(1)}, bf16[1,256,512]{2,1,0:T(8,128)(2,1)S(1)}, u32[]{:S(2)}, u32[]{:S(2)}) collective-permute-start(bf16[1,256,512]{2,1,0:T(8,128)(2,1)S(1)} %copy-done.11), channel_id=1, source_target_pairs={{0,1},{1,0},{2,3},{3,2},{4,5},{5,4},{6,7},{7,6},{8,9},{9,8},{10,11... | collective-permute-start | bytes 786440 | tf_op jit(solution)/shard_map/ppermute | solution.py:30
  161.5 1.5 copy-start
  (5 other events, 3.3 us)

commit v4 on v3

--- a/solution.py
+++ b/solution.py
@@ -54,7 +54,7 @@
 
 def stats_kernel(first, pieces, gaps_ref, uk_ref, uv_ref, q_ref, do_ref, *refs):
     lat_refs = refs[:pieces]
-    k2_ref, v_ref, st_ref = refs[-3:]
+    k2_ref, gp_ref, st_ref = refs[-3:]
     rb = lat_refs[0].shape[0]
     qn = q_ref.shape[0]
     step_heads = range(q_ref.shape[1] // HD)
@@ -73,9 +73,9 @@
             k2 = jnp.concatenate([hi, lo], axis=1)
             v = kv[:, HD:].astype(BF16)
             k2_ref[a, rows, :] = k2
-            v_ref[a, rows, :] = v
             s = masked(dot(k2, qq[a], NT), gaps_ref[first + i])
             gp = dot(v, do[a], NT)
+            gp_ref[a, rows, :] = gp
             m = jnp.maximum(jnp.max(s, axis=0, keepdims=True), -1e30)
             w = jnp.exp2(s - m)
             parts[a].append((m, jnp.sum(w, axis=0, keepdims=True), jnp.sum(w * gp, axis=0, keepdims=True)))
@@ -99,7 +99,7 @@
         functools.partial(stats_kernel, first, len(pieces)),
         out_shape=(
             jax.ShapeDtypeStruct((heads, rows, 2 * HD), BF16),
-            jax.ShapeDtypeStruct((heads, rows, HD), BF16),
+            jax.ShapeDtypeStruct((heads, rows, qn), F32),
             jax.ShapeDtypeStruct((heads // PAIR, 8, qn), F32),
         ),
         grid_spec=pltpu.PrefetchScalarGridSpec(
@@ -115,7 +115,7 @@
             + [st_spec] * len(extra),
             out_specs=[
                 pl.BlockSpec((WIDE, rows, 2 * HD), lambda g, *_: (g, 0, 0)),
-                pl.BlockSpec((WIDE, rows, HD), lambda g, *_: (g, 0, 0)),
+                pl.BlockSpec((WIDE, rows, qn), lambda g, *_: (g, 0, 0)),
                 st_spec,
             ],
         ),
@@ -140,7 +140,7 @@
         delta.append(d / t)
     gq = [jnp.zeros((qn, 2 * HD), F32) for a in pair]
     base = 0
-    for chunk, k2_ref, v_ref, lower, size in blocks:
+    for chunk, k2_ref, gp_ref, lower, size in blocks:
         rb = size // 2
         here, rows = pl.ds(lower, size), pl.ds(base, size)
         for a in pair:
@@ -149,7 +149,7 @@
             s = jnp.concatenate(
                 [masked(s[:rb], gaps_ref[2 * chunk]), masked(s[rb:], gaps_ref[2 * chunk + 1])], axis=0
             )
-            gp = dot(v_ref[a, here, :], do[a], NT)
+            gp = gp_ref[a, here, :]
             p = jnp.exp2(s - shift[a])
             ds = (p * (gp - delta[a]) * SCALE).astype(BF16)
             low = p.astype(BF16)
@@ -202,19 +202,19 @@
 
 def far_kernel(n, chunks, gaps_ref, q_ref, do_ref, *refs):
     st_refs, refs = refs[:n], refs[n:]
-    k_refs, v_refs, refs = refs[: len(chunks)], refs[len(chunks) : 2 * len(chunks)], refs[2 * len(chunks) :]
+    k_refs, gp_refs, refs = refs[: len(chunks)], refs[len(chunks) : 2 * len(chunks)], refs[2 * len(chunks) :]
     uk_ref, uv_ref, uk2_ref, uv2_ref, ok_ref, ov_ref, gk_ref, gv_ref, gq_ref, keep_ref, send_ref, gl_ref = refs
-    blocks = [(c, k, v, 0, k.shape[1]) for c, k, v in zip(chunks, k_refs, v_refs)]
+    blocks = [(c, k, v, 0, k.shape[1]) for c, k, v in zip(chunks, k_refs, gp_refs)]
     gq_ref[...] = head_grads(gaps_ref, q_ref, do_ref, st_refs, blocks, gk_ref, gv_ref)
     add_latent(gl_ref, (gk_ref, gv_ref, uk_ref, uv_ref), (ok_ref, ov_ref, uk2_ref, uv2_ref), keep_ref, send_ref)
 
 
 def near_kernel(n, chunks, gaps_ref, q_ref, do_ref, *refs):
     st_refs, refs = refs[:n], refs[n:]
-    k_refs, v_refs, refs = refs[: len(chunks)], refs[len(chunks) : 2 * len(chunks)], refs[2 * len(chunks) :]
+    k_refs, gp_refs, refs = refs[: len(chunks)], refs[len(chunks) : 2 * len(chunks)], refs[2 * len(chunks) :]
     uk_ref, uv_ref, uk2_ref, uv2_ref, ok_ref, ov_ref, latt_ref, fk_ref, fv_ref, fq_ref = refs[:10]
     out_ref, keep_ref, send_ref, gk_ref, gv_ref, gl_ref = refs[10:]
-    blocks = [(c, k, v, 0, k.shape[1]) for c, k, v in zip(chunks, k_refs, v_refs)]
+    blocks = [(c, k, v, 0, k.shape[1]) for c, k, v in zip(chunks, k_refs, gp_refs)]
     gq = fq_ref[...] + head_grads(gaps_ref, q_ref, do_ref, st_refs, blocks, gk_ref, gv_ref)
     rest = fk_ref.shape[0]
     terms = [
@@ -304,7 +304,7 @@
     picked = [rows_of(c) for c in chunks]
     in_specs = [pl.BlockSpec((qn, wide), own)] * 2 + [pl.BlockSpec((None, 8, qn), own3)] * n
     in_specs += [pl.BlockSpec((PAIR, size, 2 * HD), index) for _, index in picked]
-    in_specs += [pl.BlockSpec((PAIR, size, HD), index) for _, index in picked]
+    in_specs += [pl.BlockSpec((PAIR, size, qn), index) for _, index in picked]
     in_specs += [pl.BlockSpec((depth, wide), own)] * 2 + [pl.BlockSpec((depth, span), col)] * 2
     in_specs += [pl.BlockSpec((rows, span), lambda g, *_: (0 if far else other[0].shape[0] // rows - 1, g))] * 2
     grads = (jax.ShapeDtypeStruct((rows, cols), BF16),) * 2
@@ -394,8 +394,9 @@
     )
     outs.append(lax.all_to_all(after(part, outs[0]), "ctx", 0, 0, tiled=True))
     got = [swap(far[k], "head", 2 * (near + k)) for k in range(chunks - near)]
-    close = close.astype(F32) + swap(after(close_away, outs[1], *got), "head", 1).astype(F32)
+    close = close.astype(F32) + swap(close_away, "head", 1).astype(F32)
     grad_latent = close[0]
+    *got, outs[1] = lax.optimization_barrier((*got, outs[1]))
     for x in got:
         grad_latent = grad_latent + x.astype(F32)
 

time: 165 us -> 163 us (0.988)
  starting transfers between devices: 22.4 us -> 20.5 us
    all_to_all x1, waiting for transfers between devices: 13 us -> 7.66 us  [local(): outs.append(lax.all_to_all(after(part, outs[0]), 'ctx', 0, 0, tiled=True))]
    ppermute x15, waiting for transfers between devices: 16.3 us -> 20.1 us  [swap(): return lax.ppermute(array, axis, [(i, i ^ distance) for i in range(count)])]
    pallas_call x2, Pallas kernels: 29.5 us -> 32.3 us  [run_stats(): pl.pallas_call(functools.partial(stats_kernel, first, len(pieces)), out_s...]
    pallas_call x1, Pallas kernels: 31.6 us -> 29.3 us  [run_whole(): pl.pallas_call(functools.partial(whole_kernel, n, len(held)), out_shape=(...]
    ppermute x15, starting transfers between devices: 13.9 us -> 11.9 us  [swap(): return lax.ppermute(array, axis, [(i, i ^ distance) for i in range(count)])]
  transfers between devices with their start and end apart: 17 -> 17, of which waited for: 7 -> 9; matrix products, arithmetic and copies ran while one was open for 5% -> 5% of each run, Pallas kernels for 26% -> 27%
where the time goes in v4:
time: 163 us; the launch traced here: 162 us
  Pallas kernels  94.9 us (58%)
  waiting for transfers between devices  33.2 us (20%)
  starting transfers between devices  20.5 us (13%)
  other arithmetic  9.17 us (6%)
  local copies, waits for them, and re-layouts  3.46 us (2%)
    pallas_call x2, Pallas kernels, run_stats(): pl.pallas_call(functools.partial(stats_kernel, first, len(pieces)), out_s...  32.3 us
    pallas_call x2, Pallas kernels, run_split(): pl.pallas_call(functools.partial(kernel, n, chunks), out_shape=out_shape,...  29.8 us
    pallas_call x1, Pallas kernels, run_whole(): pl.pallas_call(functools.partial(whole_kernel, n, len(held)), out_shape=(...  29.3 us
    ppermute x15, waiting for transfers between devices, swap(): return lax.ppermute(array, axis, [(i, i ^ distance) for i in range(count)])  20.1 us
    ppermute x15, starting transfers between devices, swap(): return lax.ppermute(array, axis, [(i, i ^ distance) for i in range(count)])  11.9 us
    all_to_all x1, waiting for transfers between devices, local(): outs.append(lax.all_to_all(after(part, outs[0]), 'ctx', 0, 0, tiled=True))  7.66 us
    all_to_all x1, waiting for transfers between devices, local(): outs.append(lax.all_to_all(part, 'ctx', 0, 0, tiled=True))  5.37 us
    all_to_all x1, starting transfers between devices, local(): outs.append(lax.all_to_all(part, 'ctx', 0, 0, tiled=True))  5.04 us
  transfers between devices with their start and end apart: 17, of which 9 were waited for; matrix products, arithmetic and copies ran while one was open for 5% of the time, Pallas kernels for 27%

profile of v4, /device:TPU:17, one launch (start us, length us, event | category | flops | bytes accessed | tf_op | source)
XLA Modules:
  0.0 162.0 jit_solution(4623554594388206395)
XLA Ops:
  1.4 1.4 collective-permute-start
  2.7 1.3 collective-permute-start.5
  5.3 11.1 %stats.2 = (bf16[16,512,256]{2,1,0:T(8,128)(2,1)}, f32[16,512,256]{2,1,0:T(8,128)}, f32[8,8,256]{2,1,0:T(8,128)}) custom-call(s32[8]{0:T(128)} %multiply_subtract_fusion.gaps_ref, bf16[512,2048]{1,0:T(8,128)(2,1)} %refs_8_.1, bf16[512,2048]{1,0:T(8,128)(2,1)} %refs_9_.1, bf16[256,2048]{1,0:T(8,128)(2,1)} %q_ref.9, bf16[256,2048]{1,0:T(8,128)(2,1)} %do_ref.9, ...), custom_call_target="tpu_custom_call" | custom-call | flops 4294967296 | bytes 6291456 | tf_op jit(solution)/shard_map/stats/pallas_call | solution.py:98
  16.4 11.2 %collective-permute-done.5.refs_4_ = bf16[256,512]{1,0:T(8,128)(2,1)S(1)} collective-permute-done((bf16[256,512]{1,0:T(8,128)(2,1)}, bf16[256,512]{1,0:T(8,128)(2,1)S(1)}, u32[]{:S(2)}, u32[]{:S(2)}) %collective-permute-start.5) | collective-permute-done | bytes 262176 | tf_op jit(solution)/shard_map/ppermute | solution.py:30
  31.1 21.2 %stats.3 = (bf16[16,1536,256]{2,1,0:T(8,128)(2,1)}, f32[16,1536,256]{2,1,0:T(8,128)}, f32[8,8,256]{2,1,0:T(8,128)}) custom-call(s32[8]{0:T(128)} %multiply_subtract_fusion.gaps_ref, bf16[512,2048]{1,0:T(8,128)(2,1)} %refs_8_.1, bf16[512,2048]{1,0:T(8,128)(2,1)} %refs_9_.1, bf16[256,2048]{1,0:T(8,128)(2,1)} %q_ref.9, bf16[256,2048]{1,0:T(8,128)(2,1)} %do_ref.9, ...), custom_call_target="tpu_custom_call" | custom-call | flops 12884901888 | bytes 18874368 | tf_op jit(solution)/shard_map/stats/pallas_call | solution.py:98
  52.3 2.2 %collective-permute-start.9 = (f32[8,8,256]{2,1,0:T(8,128)}, f32[8,8,256]{2,1,0:T(8,128)S(1)}, u32[]{:S(2)}, u32[]{:S(2)}) collective-permute-start(f32[8,8,256]{2,1,0:T(8,128)} %get-tuple-element.35.refs_0_), channel_id=1, source_target_pairs={{0,24},{8,16},{16,8},{24,0},{1,25},{9,17},{17,9},{25,1},{2,26},{10... | collective-permute-start | bytes 196616 | tf_op jit(solution)/shard_map/ppermute | solution.py:30
  55.0 3.5 %turn.1.refs_8_.refs_12_ = bf16[512,2048]{1,0:T(8,128)(2,1)} custom-call(bf16[256,512]{1,0:T(8,128)(2,1)} %copy-done.6, bf16[256,512]{1,0:T(8,128)(2,1)} %copy-done.8, bf16[256,512]{1,0:T(8,128)(2,1)} %copy-done.5, bf16[256,512]{1,0:T(8,128)(2,1)} %copy-done.9, bf16[256,512]{1,0:T(8,128)(2,1)} %copy-done.7, bf16[256,512]{1,0:T(8,128)(2,1)} %copy-done.10, ...), custom_call_target="tpu_custom_call" | custom-call | tf_op jit(solution)/shard_map/turn/pallas_call | solution.py:236
  59.2 29.3 %whole.1 = (bf16[2048,1536]{1,0:T(8,128)(2,1)}, bf16[2048,1536]{1,0:T(8,128)(2,1)}, bf16[4,160,3072]{2,1,0:T(8,128)(2,1)}) custom-call(s32[8]{0:T(128)} %multiply_subtract_fusion.gaps_ref, bf16[256,2048]{1,0:T(8,128)(2,1)} %q_ref.9, bf16[256,2048]{1,0:T(8,128)(2,1)} %do_ref.9, f32[8,8,256]{2,1,0:T(8,128)} %get-tuple-element.35.refs_0_, ...), custom_call_target="tpu_custom_call" | custom-call | flops 17716740096 | bytes 31457280 | tf_op jit(solution)/shard_map/whole/pallas_call | solution.py:259
  88.6 5.0 %all-to-all-start = ((bf16[4,160,3072]{2,1,0:T(8,128)(2,1)}), bf16[4,160,3072]{2,1,0:T(8,128)(2,1)}, u32[]{:S(2)}, u32[]{:S(2)}) async-start(bf16[4,160,3072]{2,1,0:T(8,128)(2,1)} %get-tuple-element.41), calls=%async_computation | async-start | bytes 7864320 | tf_op jit(solution)/shard_map/all_to_all | solution.py:386
  93.6 17.7 %far.1 = (bf16[1536,512]{1,0:T(8,128)(2,1)}, bf16[1536,512]{1,0:T(8,128)(2,1)}, f32[256,512]{1,0:T(8,128)}, bf16[3,256,512]{2,1,0:T(8,128)(2,1)}, bf16[3,256,512]{2,1,0:T(8,128)(2,1)}) custom-call(s32[8]{0:T(128)} %multiply_subtract_fusion.gaps_ref, bf16[256,2048]{1,0:T(8,128)(2,1)} %q_ref.9, bf16[256,2048]{1,0:T(8,128)(2,1)} %do_ref.9, ...), custom_call_target="tpu_custom_call" | custom-call | flops 10871635968 | bytes 7864320 | tf_op jit(solution)/shard_map/far/pallas_call | solution.py:328
  111.3 1.7 %collective-permute-start.10 = (bf16[3,256,512]{2,1,0:T(8,128)(2,1)}, bf16[3,256,512]{2,1,0:T(8,128)(2,1)S(1)}, u32[]{:S(2)}, u32[]{:S(2)}) collective-permute-start(bf16[3,256,512]{2,1,0:T(8,128)(2,1)} %get-tuple-element.45), channel_id=1, source_target_pairs={{0,1},{1,0},{2,3},{3,2},{4,5},{5,4},{6,7},{7,6},{8,9},{9,8},{10,11... | collective-permute-start | bytes 2359304 | tf_op jit(solution)/shard_map/ppermute | solution.py:30
  113.0 2.1 %collective-permute-done.10 = bf16[3,256,512]{2,1,0:T(8,128)(2,1)S(1)} collective-permute-done((bf16[3,256,512]{2,1,0:T(8,128)(2,1)}, bf16[3,256,512]{2,1,0:T(8,128)(2,1)S(1)}, u32[]{:S(2)}, u32[]{:S(2)}) %collective-permute-start.10) | collective-permute-done | bytes 786464 | tf_op jit(solution)/shard_map/ppermute | solution.py:30
  115.1 1.3 add_convert_fusion
  116.5 12.1 %near.1 = (bf16[4,160,1024]{2,1,0:T(8,128)(2,1)}, bf16[1,256,512]{2,1,0:T(8,128)(2,1)}, bf16[1,256,512]{2,1,0:T(8,128)(2,1)}) custom-call(s32[8]{0:T(128)} %multiply_subtract_fusion.gaps_ref, bf16[256,2048]{1,0:T(8,128)(2,1)} %q_ref.9, bf16[256,2048]{1,0:T(8,128)(2,1)} %do_ref.9, f32[8,8,256]{2,1,0:T(8,128)} %get-tuple-element.35.refs_0_, ...), custom_call_target="tpu_custom_call" | custom-call | flops 3623878656 | bytes 2621440 | tf_op jit(solution)/shard_map/near/pallas_call | solution.py:328
  129.0 0.9 slice_bitcast_fusion
  129.9 2.6 %collective-permute-start.11 = (bf16[256,512]{1,0:T(8,128)(2,1)}, bf16[256,512]{1,0:T(8,128)(2,1)}, u32[]{:S(2)}, u32[]{:S(2)}) collective-permute-start(bf16[256,512]{1,0:T(8,128)(2,1)} %get-tuple-element.64), channel_id=1, source_target_pairs={{0,2},{1,3},{2,0},{3,1},{4,6},{5,7},{6,4},{7,5},{8,10},{9,11},{10,... | collective-permute-start | bytes 786440 | tf_op jit(solution)/shard_map/ppermute | solution.py:30
  132.5 5.4 %all-to-all-done = bf16[4,160,3072]{2,1,0:T(8,128)(2,1)} async-done(((bf16[4,160,3072]{2,1,0:T(8,128)(2,1)}), bf16[4,160,3072]{2,1,0:T(8,128)(2,1)}, u32[]{:S(2)}, u32[]{:S(2)}) %all-to-all-start) | async-done | bytes 3932192 | tf_op jit(solution)/shard_map/all_to_all | solution.py:386
  137.9 3.5 %all-to-all-start.1 = ((bf16[4,160,1024]{2,1,0:T(8,128)(2,1)}), bf16[4,160,1024]{2,1,0:T(8,128)(2,1)S(1)}, u32[]{:S(2)}, u32[]{:S(2)}) async-start(bf16[4,160,1024]{2,1,0:T(8,128)(2,1)} %get-tuple-element.51), calls=%async_computation.1 | async-start | bytes 2621440 | tf_op jit(solution)/shard_map/all_to_all | solution.py:395
  141.5 2.7 %add_bitcast_fusion = f32[160,3072]{1,0:T(8,128)S(1)} fusion(bf16[4,160,3072]{2,1,0:T(8,128)(2,1)} %all-to-all-done), kind=kLoop, calls=%fused_computation | loop fusion | flops 3440640 | bytes 5898240 | tf_op jit(solution)/shard_map/add | solution.py:403
  144.3 1.7 %collective-permute-done.13 = bf16[256,512]{1,0:T(8,128)(2,1)} collective-permute-done((bf16[256,512]{1,0:T(8,128)(2,1)}, bf16[256,512]{1,0:T(8,128)(2,1)}, u32[]{:S(2)}, u32[]{:S(2)}) %collective-permute-start.13) | collective-permute-done | bytes 262176 | tf_op jit(solution)/shard_map/ppermute | solution.py:30
  146.0 3.6 %collective-permute-done.12 = bf16[256,512]{1,0:T(8,128)(2,1)} collective-permute-done((bf16[256,512]{1,0:T(8,128)(2,1)}, bf16[256,512]{1,0:T(8,128)(2,1)}, u32[]{:S(2)}, u32[]{:S(2)}) %collective-permute-start.12) | collective-permute-done | bytes 262176 | tf_op jit(solution)/shard_map/ppermute | solution.py:30
  149.7 7.7 %all-to-all-done.1 = bf16[4,160,1024]{2,1,0:T(8,128)(2,1)S(1)} async-done(((bf16[4,160,1024]{2,1,0:T(8,128)(2,1)}), bf16[4,160,1024]{2,1,0:T(8,128)(2,1)S(1)}, u32[]{:S(2)}, u32[]{:S(2)}) %all-to-all-start.1) | async-done | bytes 1310752 | tf_op jit(solution)/shard_map/all_to_all | solution.py:395
  158.4 1.5 pad_maximum_fusion
  159.9 2.1 %fusion.1 = f32[256,512]{1,0:T(8,128)} fusion(bf16[256,512]{1,0:T(8,128)(2,1)} %collective-permute-done.13, bf16[256,512]{1,0:T(8,128)(2,1)} %collective-permute-done.12, bf16[256,512]{1,0:T(8,128)(2,1)} %collective-permute-done.11, bf16[1,256,512]{2,1,0:T(8,128)(2,1)S(1)} %collective-permute-done.14, bf16[1,256,512]{2,1,0:T(8,128)(2,1)S(1)} %copy-done.3), kind=kLoop, calls=%fused_computation.8 | loop fusion | flops 1179648 | bytes 1835008 | tf_op jit(solution)/shard_map/add | solution.py:401
  (50 shorter events, 8.2 us)
Async XLA Ops:
  0.6 4.0 %collective-permute-start.1 = (bf16[256,512]{1,0:T(8,128)(2,1)}, bf16[256,512]{1,0:T(8,128)(2,1)S(1)}, u32[]{:S(2)}, u32[]{:S(2)}) collective-permute-start(bf16[256,512]{1,0:T(8,128)(2,1)} %refs_6_.2), channel_id=1, source_target_pairs={{0,1},{1,0},{2,3},{3,2},{4,5},{5,4},{6,7},{7,6},{8,9},{9,8},{10,11... | collective-permute-start | bytes 786440 | tf_op jit(solution)/shard_map/ppermute | solution.py:30
  1.4 26.3 %collective-permute-start.3 = (bf16[256,512]{1,0:T(8,128)(2,1)}, bf16[256,512]{1,0:T(8,128)(2,1)S(1)}, u32[]{:S(2)}, u32[]{:S(2)}) collective-permute-start(bf16[256,512]{1,0:T(8,128)(2,1)} %refs_6_.2), channel_id=1, source_target_pairs={{0,4},{1,5},{2,6},{3,7},{4,0},{5,1},{6,2},{7,3},{8,12},{9,13},{10,... | collective-permute-start | bytes 786440 | tf_op jit(solution)/shard_map/ppermute | solution.py:30
  1.4 26.3 %collective-permute-start = (bf16[256,512]{1,0:T(8,128)(2,1)}, bf16[256,512]{1,0:T(8,128)(2,1)S(1)}, u32[]{:S(2)}, u32[]{:S(2)}) collective-permute-start(bf16[256,512]{1,0:T(8,128)(2,1)} %refs_6_.2), channel_id=1, source_target_pairs={{0,2},{1,3},{2,0},{3,1},{4,6},{5,7},{6,4},{7,5},{8,10},{9,11},{10,... | collective-permute-start | bytes 786440 | tf_op jit(solution)/shard_map/ppermute | solution.py:30
  2.7 24.9 %collective-permute-start.5 = (bf16[256,512]{1,0:T(8,128)(2,1)}, bf16[256,512]{1,0:T(8,128)(2,1)S(1)}, u32[]{:S(2)}, u32[]{:S(2)}) collective-permute-start(bf16[256,512]{1,0:T(8,128)(2,1)} %refs_6_.2), channel_id=1, source_target_pairs={{0,6},{1,7},{2,4},{3,5},{4,2},{5,3},{6,0},{7,1},{8,14},{9,15},{10,... | collective-permute-start | bytes 786440 | tf_op jit(solution)/shard_map/ppermute | solution.py:30
  4.6 0.7 copy-start.4
  27.6 2.5 %copy-start.7 = (bf16[256,512]{1,0:T(8,128)(2,1)}, bf16[256,512]{1,0:T(8,128)(2,1)S(1)}, u32[]{:S(2)}) copy-start(bf16[256,512]{1,0:T(8,128)(2,1)S(1)} %collective-permute-done.5.refs_4_) | copy-start | bytes 786436
  27.6 2.4 %copy-start.5 = (bf16[256,512]{1,0:T(8,128)(2,1)}, bf16[256,512]{1,0:T(8,128)(2,1)S(1)}, u32[]{:S(2)}) copy-start(bf16[256,512]{1,0:T(8,128)(2,1)S(1)} %collective-permute-done.3.refs_2_) | copy-start | bytes 786436
  27.6 2.4 %copy-start.6 = (bf16[256,512]{1,0:T(8,128)(2,1)}, bf16[256,512]{1,0:T(8,128)(2,1)S(1)}, u32[]{:S(2)}) copy-start(bf16[256,512]{1,0:T(8,128)(2,1)S(1)} %collective-permute-done.refs_0_) | copy-start | bytes 786436
  27.7 1.7 %collective-permute-start.2 = (bf16[256,512]{1,0:T(8,128)(2,1)S(1)}, bf16[256,512]{1,0:T(8,128)(2,1)S(1)}, u32[]{:S(2)}, u32[]{:S(2)}) collective-permute-start(bf16[256,512]{1,0:T(8,128)(2,1)S(1)} %collective-permute-done.refs_0_), channel_id=1, source_target_pairs={{0,1},{1,0},{2,3},{3,2},{4,5},{5,4},{6,7},{7,6},{8,9},{9,8},{10,11... | collective-permute-start | bytes 786440 | tf_op jit(solution)/shard_map/ppermute | solution.py:30
  28.2 1.5 collective-permute-start.4
  28.2 1.8 %collective-permute-start.6 = (bf16[256,512]{1,0:T(8,128)(2,1)S(1)}, bf16[256,512]{1,0:T(8,128)(2,1)S(1)}, u32[]{:S(2)}, u32[]{:S(2)}) collective-permute-start(bf16[256,512]{1,0:T(8,128)(2,1)S(1)} %collective-permute-done.5.refs_4_), channel_id=1, source_target_pairs={{0,1},{1,0},{2,3},{3,2},{4,5},{5,4},{6,7},{7,6},{8,9},{9,8},{10,11... | collective-permute-start | bytes 786440 | tf_op jit(solution)/shard_map/ppermute | solution.py:30
  29.3 0.8 copy-start.8
  30.4 0.7 copy-start.10
  52.3 6.2 %collective-permute-start.9 = (f32[8,8,256]{2,1,0:T(8,128)}, f32[8,8,256]{2,1,0:T(8,128)S(1)}, u32[]{:S(2)}, u32[]{:S(2)}) collective-permute-start(f32[8,8,256]{2,1,0:T(8,128)} %get-tuple-element.35.refs_0_), channel_id=1, source_target_pairs={{0,24},{8,16},{16,8},{24,0},{1,25},{9,17},{17,9},{25,1},{2,26},{10... | collective-permute-start | bytes 196616 | tf_op jit(solution)/shard_map/ppermute | solution.py:30
  54.6 4.0 %collective-permute-start.8 = (f32[8,8,256]{2,1,0:T(8,128)}, f32[8,8,256]{2,1,0:T(8,128)S(1)}, u32[]{:S(2)}, u32[]{:S(2)}) collective-permute-start(f32[8,8,256]{2,1,0:T(8,128)} %get-tuple-element.35.refs_0_), channel_id=1, source_target_pairs={{0,16},{8,24},{16,0},{24,8},{1,17},{9,25},{17,1},{25,9},{2,18},{10... | collective-permute-start | bytes 196616 | tf_op jit(solution)/shard_map/ppermute | solution.py:30
  54.8 3.8 %collective-permute-start.7 = (f32[8,8,256]{2,1,0:T(8,128)}, f32[8,8,256]{2,1,0:T(8,128)S(1)}, u32[]{:S(2)}, u32[]{:S(2)}) collective-permute-start(f32[8,8,256]{2,1,0:T(8,128)} %get-tuple-element.35.refs_0_), channel_id=1, source_target_pairs={{0,8},{8,0},{16,24},{24,16},{1,9},{9,1},{17,25},{25,17},{2,10},{10... | collective-permute-start | bytes 196616 | tf_op jit(solution)/shard_map/ppermute | solution.py:30
  88.6 49.4 %all-to-all-start = ((bf16[4,160,3072]{2,1,0:T(8,128)(2,1)}), bf16[4,160,3072]{2,1,0:T(8,128)(2,1)}, u32[]{:S(2)}, u32[]{:S(2)}) async-start(bf16[4,160,3072]{2,1,0:T(8,128)(2,1)} %get-tuple-element.41), calls=%async_computation | async-start | bytes 7864320 | tf_op jit(solution)/shard_map/all_to_all | solution.py:386
  111.3 3.8 %collective-permute-start.10 = (bf16[3,256,512]{2,1,0:T(8,128)(2,1)}, bf16[3,256,512]{2,1,0:T(8,128)(2,1)S(1)}, u32[]{:S(2)}, u32[]{:S(2)}) collective-permute-start(bf16[3,256,512]{2,1,0:T(8,128)(2,1)} %get-tuple-element.45), channel_id=1, source_target_pairs={{0,1},{1,0},{2,3},{3,2},{4,5},{5,4},{6,7},{7,6},{8,9},{9,8},{10,11... | collective-permute-start | bytes 2359304 | tf_op jit(solution)/shard_map/ppermute | solution.py:30
  128.6 31.3 %collective-permute-start.14 = (bf16[1,256,512]{2,1,0:T(8,128)(2,1)}, bf16[1,256,512]{2,1,0:T(8,128)(2,1)S(1)}, u32[]{:S(2)}, u32[]{:S(2)}) collective-permute-start(bf16[1,256,512]{2,1,0:T(8,128)(2,1)} %get-tuple-element.54), channel_id=1, source_target_pairs={{0,1},{1,0},{2,3},{3,2},{4,5},{5,4},{6,7},{7,6},{8,9},{9,8},{10,11... | collective-permute-start | bytes 786440 | tf_op jit(solution)/shard_map/ppermute | solution.py:30
  129.9 16.1 %collective-permute-start.13 = (bf16[256,512]{1,0:T(8,128)(2,1)}, bf16[256,512]{1,0:T(8,128)(2,1)}, u32[]{:S(2)}, u32[]{:S(2)}) collective-permute-start(bf16[256,512]{1,0:T(8,128)(2,1)} %get-tuple-element.62), channel_id=1, source_target_pairs={{0,6},{1,7},{2,4},{3,5},{4,2},{5,3},{6,0},{7,1},{8,14},{9,15},{10,... | collective-permute-start | bytes 786440 | tf_op jit(solution)/shard_map/ppermute | solution.py:30
  129.9 19.8 %collective-permute-start.12 = (bf16[256,512]{1,0:T(8,128)(2,1)}, bf16[256,512]{1,0:T(8,128)(2,1)}, u32[]{:S(2)}, u32[]{:S(2)}) collective-permute-start(bf16[256,512]{1,0:T(8,128)(2,1)} %get-tuple-element.63), channel_id=1, source_target_pairs={{0,4},{1,5},{2,6},{3,7},{4,0},{5,1},{6,2},{7,3},{8,12},{9,13},{10,... | collective-permute-start | bytes 786440 | tf_op jit(solution)/shard_map/ppermute | solution.py:30
  129.9 19.8 %collective-permute-start.11 = (bf16[256,512]{1,0:T(8,128)(2,1)}, bf16[256,512]{1,0:T(8,128)(2,1)}, u32[]{:S(2)}, u32[]{:S(2)}) collective-permute-start(bf16[256,512]{1,0:T(8,128)(2,1)} %get-tuple-element.64), channel_id=1, source_target_pairs={{0,2},{1,3},{2,0},{3,1},{4,6},{5,7},{6,4},{7,5},{8,10},{9,11},{10,... | collective-permute-start | bytes 786440 | tf_op jit(solution)/shard_map/ppermute | solution.py:30
  137.9 19.4 %all-to-all-start.1 = ((bf16[4,160,1024]{2,1,0:T(8,128)(2,1)}), bf16[4,160,1024]{2,1,0:T(8,128)(2,1)S(1)}, u32[]{:S(2)}, u32[]{:S(2)}) async-start(bf16[4,160,1024]{2,1,0:T(8,128)(2,1)} %get-tuple-element.51), calls=%async_computation.1 | async-start | bytes 2621440 | tf_op jit(solution)/shard_map/all_to_all | solution.py:395
  158.4 1.5 copy-start.3
  (4 other events, 2.6 us)
